TPU v7x, 32 devices: a whole 2x2x4 slice. The times are simulated.
32 devices in a mesh: fsdp: 32 (over z, y, x, core).
Axes of the slice: x: 2, y: 2, z: 4, core: 2. Of those that a mesh axis runs over, the one named last changes fastest.
Arguments:
- tokens: bfloat16 [32768, 768], P('fsdp'), may hold values from -6 to 6
- mask_bits: int32 [32768], P('fsdp'), may hold values from 0 to 1, as said below
- pad_flags: int32 [128], P('fsdp'), may hold values from 0 to 1, as said below
- ln1_gain: bfloat16 [768], P('fsdp'), may hold values from 0.5 to 1.5
- ln1_bias: bfloat16 [768], P('fsdp'), may hold values from -3 to 3
- qkv_weight: bfloat16 [768, 2304], P('fsdp'), may hold values from -0.21875 to 0.21875
- qkv_bias: bfloat16 [2304], P('fsdp'), may hold values from -3 to 3
- proj_weight: bfloat16 [768, 768], P('fsdp'), may hold values from -0.875 to 0.875
- proj_bias: bfloat16 [768], P('fsdp'), may hold values from -3 to 3
- ln2_gain: bfloat16 [768], P('fsdp'), may hold values from 0.5 to 1.5
- ln2_bias: bfloat16 [768], P('fsdp'), may hold values from -3 to 3
- fc1_weight: bfloat16 [768, 3072], P('fsdp'), may hold values from -0.21875 to 0.21875
- fc1_bias: bfloat16 [3072], P('fsdp'), may hold values from -3 to 3
- fc2_weight: bfloat16 [3072, 768], P('fsdp'), may hold values from -0.21875 to 0.21875
- fc2_bias: bfloat16 [768], P('fsdp'), may hold values from -3 to 3
- mask_embed: bfloat16 [768], P('fsdp'), may hold values from -4 to 4
- out_grad: bfloat16 [32768, 768], P('fsdp'), may hold values from -6 to 6
Outputs:
- block_out: bfloat16 [32768, 768], P('fsdp')
- input_grad: float32 [32768, 768], P('fsdp')
- grad_ln1_gain: float32 [768], P('fsdp')
- grad_ln1_bias: float32 [768], P('fsdp')
- grad_qkv_weight: float32 [768, 2304], P('fsdp')
- grad_qkv_bias: float32 [2304], P('fsdp')
- grad_proj_weight: float32 [768, 768], P('fsdp')
- grad_proj_bias: float32 [768], P('fsdp')
- grad_ln2_gain: float32 [768], P('fsdp')
- grad_ln2_bias: float32 [768], P('fsdp')
- grad_fc1_weight: float32 [768, 3072], P('fsdp')
- grad_fc1_bias: float32 [3072], P('fsdp')
- grad_fc2_weight: float32 [3072, 768], P('fsdp')
- grad_fc2_bias: float32 [768], P('fsdp')
- grad_mask_embed: float32 [768], P('fsdp')
Inputs may be any that keep to these rules, and one draw needn't show every extreme that they name: `mask_bits`: each clip of 16 frames masks its tokens independently with one rate of its own between one half and one. `pad_flags`: in each clip of 16 frames the flagged frames are its last ones, at least one and at most half of the clip, a count of its own.
All inputs are finite; a program needn't handle non-finite values.
Results may differ from a plain program's by a relative error of at most 0.012.
Values may be sent and summed in bfloat16 or wider, within the bound.
A program may use at most 192 MiB of HBM per device.

v0:
```python
import jax
import jax.numpy as jnp
from jax import lax
from jax.sharding import PartitionSpec as P

HEADS = 12
HEAD_DIM = 64
WIN = 256


epsilon = 1e-06


def norm_rows(values, gain_vec, shift_vec):
    row_mean = jnp.mean(values, axis=-1, keepdims=True)
    centered = values - row_mean
    variance = jnp.mean(centered * centered, axis=-1, keepdims=True)
    return centered * lax.rsqrt(variance + epsilon) * gain_vec + shift_vec


def gelu_exact(values):
    return jax.nn.gelu(values, approximate=False)


def forward_pass(full, tok_rows, masked):
    (
        gain_one,
        shift_one,
        qkv_w,
        qkv_b,
        proj_w,
        proj_b,
        gain_two,
        shift_two,
        up_w,
        up_b,
        down_w,
        down_b,
        mask_vec,
    ) = full
    row_count = tok_rows.shape[0]
    width = tok_rows.shape[1]
    frames = row_count // WIN
    mixed_in = jnp.where(
        masked[:, None] > 0, mask_vec.astype(jnp.float32)[None, :], tok_rows.astype(jnp.float32)
    )
    normed = norm_rows(
        mixed_in, gain_one.astype(jnp.float32), shift_one.astype(jnp.float32)
    ).astype(jnp.bfloat16)
    packed = (
        jnp.dot(normed, qkv_w, preferred_element_type=jnp.float32) + qkv_b.astype(jnp.float32)
    ).astype(jnp.bfloat16)
    heads_view = packed.reshape(frames, WIN, 3, HEADS, HEAD_DIM)
    scores = jnp.einsum(
        "fqhd,fkhd->fhqk",
        heads_view[:, :, 0],
        heads_view[:, :, 1],
        preferred_element_type=jnp.float32,
    ) * HEAD_DIM ** (-0.5)
    row_max = jnp.max(scores, axis=-1, keepdims=True)
    exp_terms = jnp.exp(scores - row_max)
    row_total = jnp.sum(exp_terms, axis=-1, keepdims=True)
    probs_low = (exp_terms / row_total).astype(jnp.bfloat16)
    log_total = row_max + jnp.log(row_total)
    attended = jnp.einsum(
        "fhqk,fkhd->fqhd", probs_low, heads_view[:, :, 2], preferred_element_type=jnp.float32
    )
    attended = attended.reshape(row_count, width).astype(jnp.bfloat16)
    middle = (
        mixed_in
        + jnp.dot(attended, proj_w, preferred_element_type=jnp.float32)
        + proj_b.astype(jnp.float32)
    )
    normed_two = norm_rows(
        middle, gain_two.astype(jnp.float32), shift_two.astype(jnp.float32)
    ).astype(jnp.bfloat16)
    hidden_pre = jnp.dot(normed_two, up_w, preferred_element_type=jnp.float32) + up_b.astype(
        jnp.float32
    )
    hidden_act = gelu_exact(hidden_pre).astype(jnp.bfloat16)
    result = (
        middle
        + jnp.dot(hidden_act, down_w, preferred_element_type=jnp.float32)
        + down_b.astype(jnp.float32)
    )
    saved = (
        mixed_in,
        normed,
        packed,
        log_total,
        attended,
        middle,
        normed_two,
        hidden_pre,
        hidden_act,
    )
    return (result, saved)


def mlp_backward(full, saved, cotangent):
    (
        gain_one,
        shift_one,
        qkv_w,
        qkv_b,
        proj_w,
        proj_b,
        gain_two,
        shift_two,
        up_w,
        up_b,
        down_w,
        down_b,
        mask_vec,
    ) = full
    mixed_in, normed, packed, log_total, attended, middle, normed_two, hidden_pre, hidden_act = (
        saved
    )
    down_in = cotangent.astype(jnp.bfloat16)
    grad_down = jnp.einsum("tf,td->fd", hidden_act, down_in, preferred_element_type=jnp.float32)
    grad_down_b = jnp.sum(down_in.astype(jnp.float32), axis=0)
    grad_act = jnp.einsum("td,fd->tf", down_in, down_w, preferred_element_type=jnp.float32)
    gelu_value, gelu_pull = jax.vjp(gelu_exact, hidden_pre)
    grad_pre = gelu_pull(grad_act)[0].astype(jnp.bfloat16)
    grad_up = jnp.einsum("td,tf->df", normed_two, grad_pre, preferred_element_type=jnp.float32)
    grad_up_b = jnp.sum(grad_pre.astype(jnp.float32), axis=0)
    grad_norm_two = jnp.einsum("tf,df->td", grad_pre, up_w, preferred_element_type=jnp.float32)
    norm_value, norm_pull = jax.vjp(
        norm_rows, middle, gain_two.astype(jnp.float32), shift_two.astype(jnp.float32)
    )
    grad_middle, grad_gain_two, grad_shift_two = norm_pull(grad_norm_two)
    grad_middle = grad_middle + cotangent
    return (
        grad_middle,
        (grad_gain_two, grad_shift_two, grad_up, grad_up_b, grad_down, grad_down_b),
    )


def attn_backward(full, saved, grad_middle, masked):
    (
        gain_one,
        shift_one,
        qkv_w,
        qkv_b,
        proj_w,
        proj_b,
        gain_two,
        shift_two,
        up_w,
        up_b,
        down_w,
        down_b,
        mask_vec,
    ) = full
    mixed_in, normed, packed, log_total, attended, middle, normed_two, hidden_pre, hidden_act = (
        saved
    )
    row_count = grad_middle.shape[0]
    width = grad_middle.shape[1]
    frames = row_count // WIN
    proj_in = grad_middle.astype(jnp.bfloat16)
    grad_proj = jnp.einsum("td,te->de", attended, proj_in, preferred_element_type=jnp.float32)
    grad_proj_b = jnp.sum(proj_in.astype(jnp.float32), axis=0)
    grad_att = jnp.einsum("te,de->td", proj_in, proj_w, preferred_element_type=jnp.float32).astype(
        jnp.bfloat16
    )
    grad_att = grad_att.reshape(frames, WIN, HEADS, HEAD_DIM)
    heads_view = packed.reshape(frames, WIN, 3, HEADS, HEAD_DIM)
    query_part = heads_view[:, :, 0]
    key_part = heads_view[:, :, 1]
    value_part = heads_view[:, :, 2]
    score_scale = HEAD_DIM ** (-0.5)
    scores = (
        jnp.einsum("fqhd,fkhd->fhqk", query_part, key_part, preferred_element_type=jnp.float32)
        * score_scale
    )
    probs_full = jnp.exp(scores - log_total)
    probs_low = probs_full.astype(jnp.bfloat16)
    grad_value = jnp.einsum(
        "fhqk,fqhd->fkhd", probs_low, grad_att, preferred_element_type=jnp.float32
    )
    grad_probs = jnp.einsum(
        "fqhd,fkhd->fhqk", grad_att, value_part, preferred_element_type=jnp.float32
    )
    row_dot = jnp.sum(grad_probs * probs_full, axis=-1, keepdims=True)
    grad_scores = (probs_full * (grad_probs - row_dot)).astype(jnp.bfloat16)
    grad_query = (
        jnp.einsum("fhqk,fkhd->fqhd", grad_scores, key_part, preferred_element_type=jnp.float32)
        * score_scale
    )
    grad_key = (
        jnp.einsum("fhqk,fqhd->fkhd", grad_scores, query_part, preferred_element_type=jnp.float32)
        * score_scale
    )
    grad_packed = (
        jnp.stack([grad_query, grad_key, grad_value], axis=2)
        .reshape(row_count, 3 * width)
        .astype(jnp.bfloat16)
    )
    grad_qkv = jnp.einsum("td,te->de", normed, grad_packed, preferred_element_type=jnp.float32)
    grad_qkv_b = jnp.sum(grad_packed.astype(jnp.float32), axis=0)
    grad_normed = jnp.einsum("te,de->td", grad_packed, qkv_w, preferred_element_type=jnp.float32)
    first_value, first_pull = jax.vjp(
        norm_rows, mixed_in, gain_one.astype(jnp.float32), shift_one.astype(jnp.float32)
    )
    grad_mixed, grad_gain_one, grad_shift_one = first_pull(grad_normed)
    grad_mixed = grad_mixed + grad_middle
    chosen = masked[:, None] > 0
    tok_grad = jnp.where(chosen, 0.0, grad_mixed)
    grad_mask = jnp.sum(jnp.where(chosen, grad_mixed, 0.0), axis=0)
    return (
        tok_grad,
        (grad_gain_one, grad_shift_one, grad_qkv, grad_qkv_b, grad_proj, grad_proj_b, grad_mask),
    )


def per_device(
    tokens,
    mask_bits,
    pad_flags,
    ln1_gain,
    ln1_bias,
    qkv_weight,
    qkv_bias,
    proj_weight,
    proj_bias,
    ln2_gain,
    ln2_bias,
    fc1_weight,
    fc1_bias,
    fc2_weight,
    fc2_bias,
    mask_embed,
    out_grad,
):
    full = (
        lax.all_gather(ln1_gain, "fsdp", axis=0, tiled=True),
        lax.all_gather(ln1_bias, "fsdp", axis=0, tiled=True),
        lax.all_gather(qkv_weight, "fsdp", axis=0, tiled=True),
        lax.all_gather(qkv_bias, "fsdp", axis=0, tiled=True),
        lax.all_gather(proj_weight, "fsdp", axis=0, tiled=True),
        lax.all_gather(proj_bias, "fsdp", axis=0, tiled=True),
        lax.all_gather(ln2_gain, "fsdp", axis=0, tiled=True),
        lax.all_gather(ln2_bias, "fsdp", axis=0, tiled=True),
        lax.all_gather(fc1_weight, "fsdp", axis=0, tiled=True),
        lax.all_gather(fc1_bias, "fsdp", axis=0, tiled=True),
        lax.all_gather(fc2_weight, "fsdp", axis=0, tiled=True),
        lax.all_gather(fc2_bias, "fsdp", axis=0, tiled=True),
        lax.all_gather(mask_embed, "fsdp", axis=0, tiled=True),
    )
    result, saved = forward_pass(full, tokens, mask_bits)
    full_back = (
        lax.all_gather(ln1_gain, "fsdp", axis=0, tiled=True),
        lax.all_gather(ln1_bias, "fsdp", axis=0, tiled=True),
        lax.all_gather(qkv_weight, "fsdp", axis=0, tiled=True),
        lax.all_gather(qkv_bias, "fsdp", axis=0, tiled=True),
        lax.all_gather(proj_weight, "fsdp", axis=0, tiled=True),
        lax.all_gather(proj_bias, "fsdp", axis=0, tiled=True),
        lax.all_gather(ln2_gain, "fsdp", axis=0, tiled=True),
        lax.all_gather(ln2_bias, "fsdp", axis=0, tiled=True),
        lax.all_gather(fc1_weight, "fsdp", axis=0, tiled=True),
        lax.all_gather(fc1_bias, "fsdp", axis=0, tiled=True),
        lax.all_gather(fc2_weight, "fsdp", axis=0, tiled=True),
        lax.all_gather(fc2_bias, "fsdp", axis=0, tiled=True),
        lax.all_gather(mask_embed, "fsdp", axis=0, tiled=True),
    )
    kept_acts = forward_pass(full_back, tokens, mask_bits)[1]
    row_count = tokens.shape[0]
    frames = row_count // WIN
    frame_keep = (1 - pad_flags).astype(jnp.float32)
    tok_weight = (mask_bits.astype(jnp.float32).reshape(frames, WIN) * frame_keep[:, None]).reshape(
        row_count
    )
    cotangent = out_grad.astype(jnp.float32) * tok_weight[:, None]
    grad_middle, mlp_grads = mlp_backward(full_back, kept_acts, cotangent)
    tok_grad, attn_grads = attn_backward(full_back, kept_acts, grad_middle, mask_bits)
    shares = (
        lax.psum_scatter(attn_grads[0], "fsdp", scatter_dimension=0, tiled=True),
        lax.psum_scatter(attn_grads[1], "fsdp", scatter_dimension=0, tiled=True),
        lax.psum_scatter(attn_grads[2], "fsdp", scatter_dimension=0, tiled=True),
        lax.psum_scatter(attn_grads[3], "fsdp", scatter_dimension=0, tiled=True),
        lax.psum_scatter(attn_grads[4], "fsdp", scatter_dimension=0, tiled=True),
        lax.psum_scatter(attn_grads[5], "fsdp", scatter_dimension=0, tiled=True),
        lax.psum_scatter(mlp_grads[0], "fsdp", scatter_dimension=0, tiled=True),
        lax.psum_scatter(mlp_grads[1], "fsdp", scatter_dimension=0, tiled=True),
        lax.psum_scatter(mlp_grads[2], "fsdp", scatter_dimension=0, tiled=True),
        lax.psum_scatter(mlp_grads[3], "fsdp", scatter_dimension=0, tiled=True),
        lax.psum_scatter(mlp_grads[4], "fsdp", scatter_dimension=0, tiled=True),
        lax.psum_scatter(mlp_grads[5], "fsdp", scatter_dimension=0, tiled=True),
        lax.psum_scatter(attn_grads[6], "fsdp", scatter_dimension=0, tiled=True),
    )
    return (
        result.astype(jnp.bfloat16),
        tok_grad,
        shares[0],
        shares[1],
        shares[2],
        shares[3],
        shares[4],
        shares[5],
        shares[6],
        shares[7],
        shares[8],
        shares[9],
        shares[10],
        shares[11],
        shares[12],
    )


def solution(mesh):
    placed = (
        P("fsdp", None),
        P("fsdp"),
        P("fsdp"),
        P("fsdp"),
        P("fsdp"),
        P("fsdp", None),
        P("fsdp"),
        P("fsdp", None),
        P("fsdp"),
        P("fsdp"),
        P("fsdp"),
        P("fsdp", None),
        P("fsdp"),
        P("fsdp", None),
        P("fsdp"),
        P("fsdp"),
        P("fsdp", None),
    )
    return jax.shard_map(
        per_device,
        mesh=mesh,
        in_specs=placed,
        out_specs=(
            P("fsdp", None),
            P("fsdp", None),
            P("fsdp"),
            P("fsdp"),
            P("fsdp", None),
            P("fsdp"),
            P("fsdp", None),
            P("fsdp"),
            P("fsdp"),
            P("fsdp"),
            P("fsdp", None),
            P("fsdp"),
            P("fsdp", None),
            P("fsdp"),
            P("fsdp"),
        ),
        check_vma=False,
    )
```

profile of v0, /device:TPU:0, one launch (start us, length us, event | category | flops | bytes accessed | tf_op | source)
XLA Modules:
  0.0 820.1 jit_solution(15518555738427840588)
XLA Ops:
  19.7 43.3 %all-reduce.19 = (bf16[2304]{0:T(1024)(128)(2,1)S(1)}, bf16[768]{0:T(1024)(128)(2,1)S(1)}, bf16[768]{0:T(1024)(128)(2,1)S(1)}, bf16[768]{0:T(1024)(128)(2,1)S(1)...) all-reduce(bf16[2304]{0:T(1024)(128)(2,1)S(1)} %dynamic-update-slic, ...), channel_id=1, replica_groups=mesh['fsdp'=32] {'fsdp'}, use_global_device_ids=true, to_apply=%add.3 | all-reduce | flops 10752 | bytes 43008
  67.7 6.4 all-gather.5.cloned.1.call-done
  74.1 7.9 add_convert_fusion.1
  82.0 6.7 copy.73
  88.7 8.9 %reshape.135 = bf16[4,256,3,12,64]{1,0,4,3,2:T(4,128)(2,1)} reshape(bf16[1024,2304]{0,1:T(8,128)(2,1)} %copy.73) | data formatting | bytes 9437184 | tf_op jit(solution)/shard_map/reshape | solution.py:53
  97.6 4.1 fusion.41
  108.4 3.1 fusion.22
  114.2 15.6 %all-gather.7.cloned.1.call-done = bf16[768,768]{1,0:T(8,128)(2,1)} async-done(((bf16[24,768]{1,0:T(8,128)(2,1)}), bf16[768,768]{1,0:T(8,128)(2,1)}) %all-gather.7.cloned.1.call-update) | async-done | bytes 1179664 | tf_op jit(solution)/shard_map/all_gather | solution.py:241
  129.8 3.5 fusion.42
  135.4 59.9 %all-gather.9.cloned.1.call-done = bf16[768,3072]{1,0:T(8,128)(2,1)} async-done(((bf16[24,3072]{1,0:T(8,128)(2,1)}), bf16[768,3072]{1,0:T(8,128)(2,1)}) %all-gather.9.cloned.1.call-update) | async-done | bytes 4718608 | tf_op jit(solution)/shard_map/all_gather | solution.py:245
  195.3 37.7 %multiply_convert_fusion.1 = (bf16[1024,3072]{1,0:T(8,128)(2,1)}, f32[1024,3072]{1,0:T(8,128)}, f32[1024,3072]{1,0:T(8,128)}) fusion(f32[3072]{0:T(1024)S(1)} %convert_element_type.136, bf16[768,3072]{1,0:T(8,128)(2,1)} %all-gather.9.cloned.1.call-done, f32[1024,768]{0,1:T(8,128)} %copy-done.4, f32[768]{0:T(1024)S(1)} %convert_element_type.134, ...), kind=kOutput, calls=%fused_computation.7 | convolution fusion | flops 5043388416 | bytes 39348224 | tf_op jit(solution)/shard_map/dot_general | solution.py:77
  233.0 27.6 %all-gather.11.cloned.1.call-done = bf16[3072,768]{1,0:T(8,128)(2,1)} async-done(((bf16[96,768]{1,0:T(8,128)(2,1)}), bf16[3072,768]{1,0:T(8,128)(2,1)}) %all-gather.11.cloned.1.call-update) | async-done | bytes 4718608 | tf_op jit(solution)/shard_map/all_gather | solution.py:247
  260.6 17.2 %convert_reduce_fusion = (f32[3072]{0:T(1024)S(1)}, bf16[1024,3072]{1,0:T(8,128)(2,1)}) fusion(f32[1024,3072]{1,0:T(8,128)} %get-tuple-element.90, bf16[3072,768]{1,0:T(8,128)(2,1)} %all-gather.11.cloned.1.call-done, bf16[1024,768]{0,1:T(8,128)(2,1)S(1)} %copy.80, f32[1024]{0:T(1024)S(1)} %convert_multiply_fusion.1, f32[1024,3072]{1,0:T(8,128)} %get-tuple-element.99, ...), kind=kOutput, calls=%fused_computation.2 | convolution fusion | flops 4887671808 | bytes 37777408 | tf_op jit(solution)/shard_map/td,fd->tf/dot_general | solution.py:122
  277.8 8.4 %fusion.44 = (f32[768]{0:T(1024)S(1)}, f32[1024,768]{1,0:T(8,128)}) fusion(bf16[1024,3072]{1,0:T(8,128)(2,1)} %get-tuple-element.107, bf16[768,3072]{1,0:T(8,128)(2,1)S(1)} %copy-done.36), kind=kOutput, calls=%fused_computation.97 | convolution fusion | flops 4832623616 | bytes 14158848 | tf_op jit(solution)/shard_map/tf,df->td/dot_general | solution.py:127
  286.2 3.7 copy.81
  289.8 2.9 multiply_reduce_fusion.2
  303.6 3.0 reshape.136
  306.7 6.5 multiply_reduce_fusion
  313.2 7.3 multiply_convert_fusion
  329.8 4.5 copy.88
  338.2 6.5 fusion.36
  344.8 10.6 %fusion.34 = f32[768,3072]{1,0:T(8,128)} fusion(bf16[1024,3072]{1,0:T(8,128)(2,1)} %get-tuple-element.107, f32[1024,768]{0,1:T(8,128)} %copy-done.4, f32[768]{0:T(1024)S(1)} %convert_element_type.134, f32[768]{0:T(1024)S(1)} %convert_element_type.133, f32[1024]{0:T(1024)S(1)} %fusion.31, f32[1024]{0:T(1024)S(1)} %broadcast_multiply_fusion), kind=kOutput, calls=%fused_computation.89 | convolution fusion | flops 4835770368 | bytes 18888704 | tf_op jit(solution)/shard_map/td,tf->df/dot_general | solution.py:125
  356.8 10.4 %fusion.27 = f32[3072,768]{1,0:T(8,128)} fusion(bf16[1024,3072]{1,0:T(8,128)(2,1)} %get-tuple-element.89, bf16[1024,768]{0,1:T(8,128)(2,1)S(1)} %copy-done.13, f32[1024]{0:T(1024)S(1)} %convert_multiply_fusion.1), kind=kOutput, calls=%fused_computation.71 | convolution fusion | flops 4834197504 | bytes 17305600 | tf_op jit(solution)/shard_map/tf,td->fd/dot_general | solution.py:120
  367.9 10.0 %add_convert_fusion.2 = bf16[1024,768]{0,1:T(8,128)(2,1)} fusion(f32[1024,768]{0,1:T(8,128)} %copy-done.4, bf16[1024,3072]{1,0:T(8,128)(2,1)} %get-tuple-element.89, bf16[3072,768]{1,0:T(8,128)(2,1)} %all-gather.11.cloned.1.call-done, f32[768]{0:T(1024)S(1)} %convert_element_type.138), kind=kOutput, calls=%fused_computation.48 | convolution fusion | flops 4834197504 | bytes 15731712 | tf_op jit(solution)/shard_map/dot_general | solution.py:83
  380.6 9.1 %fusion.43 = (f32[768]{0:T(1024)S(1)}, f32[1024,768]{1,0:T(8,128)}) fusion(bf16[1024,2304]{0,1:T(8,128)(2,1)} %bitcast.74, bf16[768,2304]{1,0:T(8,128)(2,1)} %all-gather.5.cloned.1.call-done), kind=kOutput, calls=%fused_computation.96 | convolution fusion | flops 3624664320 | bytes 11406336 | tf_op jit(solution)/shard_map/te,de->td/dot_general | solution.py:202
  389.6 3.5 copy.89
  397.8 4.4 select_reduce_fusion
  402.2 40.6 %all-reduce.18 = (f32[768]{0:T(1024)S(1)}, f32[768]{0:T(1024)S(1)}, f32[2304]{0:T(1024)S(1)}, f32[768]{0:T(1024)S(1)}, f32[768]{0:T(1024)S(1)}, /*index=5*/f32[7...) all-reduce(f32[768]{0:T(1024)S(1)} %get-tuple-element.63, ...), channel_id=2, replica_groups=mesh['fsdp'=32] {'fsdp'}, use_global_device_ids=true, to_apply=%region_12.13.clone | all-reduce | flops 10752 | bytes 86016
  446.9 3.6 copy.93
  451.6 77.9 %reduce-scatter.5.cloned.1.call-done = f32[24,2304]{1,0:T(8,128)} async-done(((f32[768,2304]{1,0:T(8,128)}), f32[24,2304]{1,0:T(8,128)}) %reduce-scatter.5.cloned.1.call-update) | async-done | bytes 221200 | tf_op jit(solution)/shard_map/reduce_scatter | solution.py:280
  529.5 141.3 %reduce-scatter.9.cloned.1.call-done = f32[24,3072]{1,0:T(8,128)} async-done(((f32[768,3072]{1,0:T(8,128)}), f32[24,3072]{1,0:T(8,128)}) %reduce-scatter.9.cloned.1.call-update) | async-done | bytes 294928 | tf_op jit(solution)/shard_map/reduce_scatter | solution.py:286
  670.8 142.2 %reduce-scatter.11.cloned.1.call-done = f32[96,768]{1,0:T(8,128)} async-done(((f32[3072,768]{1,0:T(8,128)}), f32[96,768]{1,0:T(8,128)}) %reduce-scatter.11.cloned.1.call-update) | async-done | bytes 294928 | tf_op jit(solution)/shard_map/reduce_scatter | solution.py:288
  (171 shorter events, 66.8 us)
Async XLA Ops:
  7.2 66.9 %all-gather.5.cloned.1.call-start = ((), (), s32[]{:S(2)}) async-start(), calls=%async_computation.4 | async-start | bytes 3649536 | tf_op jit(solution)/shard_map/all_gather | solution.py:239
  7.9 121.9 %all-gather.7.cloned.1.call-start = ((), (), s32[]{:S(2)}) async-start(), calls=%async_computation.5 | async-start | bytes 1216512 | tf_op jit(solution)/shard_map/all_gather | solution.py:241
  8.7 186.7 %all-gather.9.cloned.1.call-start = ((), (), s32[]{:S(2)}) async-start(), calls=%async_computation.6 | async-start | bytes 4866048 | tf_op jit(solution)/shard_map/all_gather | solution.py:245
  9.4 251.2 %all-gather.11.cloned.1.call-start = ((), (), s32[]{:S(2)}) async-start(), calls=%async_computation.7 | async-start | bytes 4866048 | tf_op jit(solution)/shard_map/all_gather | solution.py:247
  10.0 441.7 %reduce-scatter.7.cloned.1.call-start = ((), (), s32[]{:S(2)}) async-start(), calls=%async_computation.9 | async-start | bytes 2433024 | tf_op jit(solution)/shard_map/reduce_scatter | solution.py:282
  11.4 118.4 %copy-start.31 = (pred[1024]{0:T(1024)(128)(4,1)}, pred[1024]{0:T(1024)(128)(4,1)S(1)}, u32[]{:S(2)}) copy-start(pred[1024]{0:T(1024)(128)(4,1)S(1)} %broadcast_compare_fusion) | copy-start | bytes 3076
  63.0 66.8 %copy-start.21 = (f32[768]{0:T(1024)}, f32[768]{0:T(1024)S(1)}, u32[]{:S(2)}) copy-start(f32[768]{0:T(1024)S(1)} %convert_element_type.121) | copy-start | bytes 9220
  63.0 11.0 %copy-start.25 = (f32[768]{0:T(1024)}, f32[768]{0:T(1024)S(1)}, u32[]{:S(2)}) copy-start(f32[768]{0:T(1024)S(1)} %convert_element_type.123) | copy-start | bytes 9220
  63.1 11.0 %copy-start.33 = (f32[768]{0:T(1024)}, f32[768]{0:T(1024)S(1)}, u32[]{:S(2)}) copy-start(f32[768]{0:T(1024)S(1)} %convert_element_type.124) | copy-start | bytes 9220
  64.8 65.0 %copy-start.1 = (bf16[1024,768]{0,1:T(8,128)(2,1)}, bf16[1024,768]{0,1:T(8,128)(2,1)S(1)}, u32[]{:S(2)}) copy-start(bf16[1024,768]{0,1:T(8,128)(2,1)S(1)} %copy.72) | copy-start | bytes 4718596
  65.3 16.7 %copy-start.23 = (f32[1024]{0:T(1024)}, f32[1024]{0:T(1024)S(1)}, u32[]{:S(2)}) copy-start(f32[1024]{0:T(1024)S(1)} %broadcast_multiply_fusion.1) | copy-start | bytes 12292
  65.9 16.1 %copy-start.27 = (f32[1024]{0:T(1024)}, f32[1024]{0:T(1024)S(1)}, u32[]{:S(2)}) copy-start(f32[1024]{0:T(1024)S(1)} %multiply_reduce_fusion.7) | copy-start | bytes 12292
  65.9 16.1 %copy-start.29 = (f32[1024]{0:T(1024)}, f32[1024]{0:T(1024)S(1)}, u32[]{:S(2)}) copy-start(f32[1024]{0:T(1024)S(1)} %fusion.30) | copy-start | bytes 12292
  67.7 192.9 %copy-start.11 = (bf16[1024,768]{0,1:T(8,128)(2,1)}, bf16[1024,768]{0,1:T(8,128)(2,1)S(1)}, u32[]{:S(2)}) copy-start(bf16[1024,768]{0,1:T(8,128)(2,1)S(1)} %copy.80) | copy-start | bytes 4718596
  103.6 4.8 copy-start
  103.6 4.8 copy-start.16
  260.6 17.2 %copy-start.36 = (bf16[768,3072]{1,0:T(8,128)(2,1)S(1)}, bf16[768,3072]{1,0:T(8,128)(2,1)}, u32[]{:S(2)}) copy-start(bf16[768,3072]{1,0:T(8,128)(2,1)} %all-gather.9.cloned.1.call-done) | copy-start | bytes 14155780
  286.2 3.7 copy-start.5
  303.6 3.1 copy-start.20
  306.7 222.9 %reduce-scatter.5.cloned.1.call-start = ((), (), s32[]{:S(2)}) async-start(), calls=%async_computation.8 | async-start | bytes 7299072 | tf_op jit(solution)/shard_map/reduce_scatter | solution.py:280
  313.2 7.3 copy-start.10
  320.6 4.0 slice-start.1
  322.6 3.5 slice-start.2
  334.3 3.9 copy-start.2
  334.3 3.9 copy-start.22
  334.3 3.9 copy-start.24
  334.4 3.8 copy-start.26
  334.4 3.8 copy-start.30
  334.4 3.8 copy-start.32
  334.4 3.8 copy-start.34
  344.7 326.1 %reduce-scatter.9.cloned.1.call-start = ((), (), s32[]{:S(2)}) async-start(), calls=%async_computation.10 | async-start | bytes 9732096 | tf_op jit(solution)/shard_map/reduce_scatter | solution.py:286
  355.4 457.6 %reduce-scatter.11.cloned.1.call-start = ((), (), s32[]{:S(2)}) async-start(), calls=%async_computation.11 | async-start | bytes 9732096 | tf_op jit(solution)/shard_map/reduce_scatter | solution.py:288
  (16 other events, 33.4 us)
Sparse Core Ops, SparseCore 0:
  10.9 63.1 all-gather.4
  77.0 52.8 all-gather.6
  132.7 62.5 all-gather.8
  198.1 62.4 all-gather.10
  306.8 97.8 reduce-scatter.6
  411.7 117.7 reduce-scatter.4
  536.0 134.7 reduce-scatter.8
  678.3 134.6 reduce-scatter.10
where the time goes:
time: 831 us; the launch traced here: 820 us
  waiting for transfers between devices  474 us (57%)
  matrix products  144 us (17%)
  blocking collectives  83.9 us (10%)
  local copies, waits for them, and re-layouts  74.8 us (9%)
  other arithmetic  28.7 us (3%)
  between operations  15 us (2%)
    reduce_scatter x1, waiting for transfers between devices, per_device(): lax.psum_scatter(mlp_grads[4], 'fsdp', scatter_dimension=0, tiled=True)  142 us
    reduce_scatter x1, waiting for transfers between devices, per_device(): lax.psum_scatter(mlp_grads[2], 'fsdp', scatter_dimension=0, tiled=True)  141 us
    unnamed x2, blocking collectives  83.9 us
    reduce_scatter x1, waiting for transfers between devices, per_device(): lax.psum_scatter(attn_grads[2], 'fsdp', scatter_dimension=0, tiled=True)  77.9 us
    all_gather x1, waiting for transfers between devices, per_device(): lax.all_gather(fc1_weight, 'fsdp', axis=0, tiled=True)  59.9 us
    dot_general x1, matrix products, forward_pass(): jnp.dot(normed_two, up_w, preferred_element_type=jnp.float32)  37.7 us
    unnamed x115, local copies, waits for them, and re-layouts  37.3 us
    all_gather x1, waiting for transfers between devices, per_device(): lax.all_gather(fc2_weight, 'fsdp', axis=0, tiled=True)  27.6 us
  transfers between devices with their start and end apart: 8, of which 7 were waited for; matrix products, arithmetic and copies ran while one was open for 23% of the time, Pallas kernels for 0%

commit v1 on v0

--- a/solution.py
+++ b/solution.py
@@ -1,6 +1,10 @@
+import functools
+
 import jax
 import jax.numpy as jnp
 from jax import lax
+from jax.experimental import pallas as pl
+from jax.experimental.pallas import tpu as pltpu
 from jax.sharding import PartitionSpec as P
 
 HEADS = 12
@@ -308,6 +312,891 @@
     )
 
 
+F32 = jnp.float32
+BF16 = jnp.bfloat16
+LANES = 128
+ROWS = 48
+COLS = 384
+PIECES = 12
+RING = 4
+MESH_ID = pl.DeviceIdType.MESH
+
+
+def dot_nn(a, b):
+    return lax.dot_general(a, b, (((1,), (0,)), ((), ())), preferred_element_type=F32)
+
+
+def dot_nt(a, b):
+    return lax.dot_general(a, b, (((1,), (1,)), ((), ())), preferred_element_type=F32)
+
+
+def dot_tn(a, b):
+    return lax.dot_general(a, b, (((0,), (0,)), ((), ())), preferred_element_type=F32)
+
+
+def row_stats(values):
+    row_mean = jnp.mean(values, axis=-1, keepdims=True)
+    centered = values - row_mean
+    return row_mean, lax.rsqrt(jnp.mean(centered * centered, axis=-1, keepdims=True) + epsilon)
+
+
+def gelu_and_slope(x):
+    phi = 0.5 + 0.5 * lax.erf(x * 0.7071067811865476)
+    return x * phi, phi + x * jnp.exp(x * x * -0.5) * 0.3989422804014327
+
+
+def norm_backward(x, row_mean, row_scale, grad, gain):
+    x_hat = (x - row_mean) * row_scale
+    prod = grad * x_hat
+    grad_gain = jnp.sum(prod, axis=0, keepdims=True)
+    grad_shift = jnp.sum(grad, axis=0, keepdims=True)
+    dx = grad * gain
+    mean_one = jnp.mean(dx, axis=-1, keepdims=True)
+    mean_two = jnp.mean(dx * x_hat, axis=-1, keepdims=True)
+    return row_scale * (dx - mean_one - x_hat * mean_two), grad_gain, grad_shift
+
+
+SMALL_ROWS = (
+    ("ln1_gain", 0, 0, 24),
+    ("ln1_bias", 0, 24, 24),
+    ("proj_bias", 0, 48, 24),
+    ("ln2_gain", 0, 72, 24),
+    ("ln2_bias", 0, 96, 24),
+    ("fc2_bias", 1, 0, 24),
+    ("mask_embed", 1, 24, 24),
+    ("qkv_bias", 1, 48, 72),
+    ("fc1_bias", 2, 0, 96),
+)
+
+
+def spread_tables(lane0, width):
+    count = 32 * width
+    k = lax.broadcasted_iota(jnp.int32, (1, count), 1)
+    pick = lax.broadcasted_iota(jnp.int32, (LANES, count), 0) == lax.rem(k, width) + lane0
+    owner = lax.broadcasted_iota(jnp.int32, (32, count), 0) == lax.div(k, width)
+    return jnp.where(pick, 1.0, 0.0).astype(BF16), owner
+
+
+SCRATCH = dict(
+    tok=((1024, 768), BF16),
+    dm=((1024, 768), BF16),
+    st=((1024, 8), F32),
+    v24=((8, 768), F32),
+    bqkv=((1, 2304), F32),
+    bfc1=((1, 3072), F32),
+    gv=((8, 768), F32),
+    gbqkv=((1, 2304), F32),
+    gbfc1=((1, 3072), F32),
+    normed=((1024, 768), BF16),
+    n2=((1024, 768), BF16),
+    tr=((768, 1024), BF16),
+    packed=((1024, 2304), BF16),
+    att=((1024, 768), BF16),
+    mid=((1024, 768), F32),
+    hact=((1024, 3072), BF16),
+    gp=((11, 768, COLS), BF16),
+    dn=((1024, 768), F32),
+    lse=((24, 8, 256), F32),
+    wa=((8, 768, COLS), BF16),
+    w1=((8, 768, COLS), BF16),
+    w2=((8, 768, COLS), BF16),
+    g2=((8, 768, COLS), BF16),
+    sv=((4, 4, 2, 16, LANES), BF16),
+    sg=((4, 4, 2, 8, LANES), F32),
+    tx=((8, 32, COLS), BF16),
+    rx=((8, 32, COLS), BF16),
+    fs=((8, ROWS, COLS), F32),
+    fr=((8, ROWS // 2, COLS), F32),
+    l0=((RING, 4, 4, ROWS, COLS), BF16),
+    l1=((RING, 2, 2, ROWS, COLS), BF16),
+    l2=((RING, 2, 4, ROWS, COLS), BF16),
+    l3=((RING, 3, ROWS, COLS), BF16),
+    s0=((4, 4, 8, LANES), F32),
+    s1=((2, 2, 8, LANES), F32),
+    s2=((2, 4, 8, LANES), F32),
+    s3=((3, 8, LANES), F32),
+)
+SEMS = dict(
+    ld=pltpu.SemaphoreType.DMA((8,)),
+    prep=pltpu.SemaphoreType.DMA((2,)),
+    ags=pltpu.SemaphoreType.DMA((PIECES + 1, 8)),
+    agr=pltpu.SemaphoreType.DMA((PIECES + 1, 8)),
+    rss=pltpu.SemaphoreType.DMA((PIECES + 1, 9)),
+    rsr=pltpu.SemaphoreType.DMA((PIECES + 1, 9)),
+    credit=pltpu.SemaphoreType.REGULAR((8,)),
+)
+
+
+class Refs:
+    pass
+
+
+def fused_kernel(*refs):
+    r = Refs()
+    names = ["tok_in", "og_in", "mask", "pad", "small", "sq", "sp", "s1w", "s2w"]
+    names += ["bo", "ig", "oq", "op", "o1", "o2", "osm"]
+    names += list(SCRATCH) + list(SEMS)
+    for name, ref in zip(names, refs):
+        setattr(r, name, ref)
+
+    me = lax.axis_index("fsdp")
+    core = lax.rem(me, 2)
+    other = 1 - core
+    chip = lax.div(me, 2)
+    xpos = lax.rem(chip, 2)
+    ypos = lax.rem(lax.div(chip, 2), 2)
+    zpos = lax.div(chip, 4)
+    xy = lax.rem(chip, 4)
+    xy_x = xy + 1 - 2 * xpos
+    xy_y = xy + 2 - 4 * ypos
+    xy_d = xy_x + 2 - 4 * ypos
+    sib = me + 1 - 2 * core
+    x_dev = me + 2 - 4 * xpos
+    y_dev = me + 4 - 8 * ypos
+
+    def z_of(k):
+        return lax.rem(zpos + k, 4)
+
+    def z_dev(k):
+        return me + 8 * (z_of(k) - zpos)
+
+    def remote(src, dst, ssem, rsem, dev):
+        return pltpu.make_async_remote_copy(
+            src_ref=src,
+            dst_ref=dst,
+            send_sem=ssem,
+            recv_sem=rsem,
+            device_id=(dev,),
+            device_id_type=MESH_ID,
+        )
+
+    wa_v = r.wa.reshape(2, 4, 4, 4, ROWS, COLS)
+    w1_v = r.w1.reshape(2, 4, 4, 4, ROWS, COLS)
+    w2_v = r.w2.reshape(2, 4, 4, 2, 2, ROWS, COLS)
+    w2_shard = r.w2.reshape(2, 4, 4, 2, 2 * ROWS, COLS)
+    w2_m = r.w2.reshape(2, 3072, COLS)
+    wa_m = r.wa.reshape(2, 4, 768, COLS)
+    w1_m = r.w1.reshape(2, 4, 768, COLS)
+    g2_v = r.g2.reshape(2, 4, 4, 2, 2, ROWS, COLS)
+    g2_m = r.g2.reshape(2, 3072, COLS)
+    ga_v = r.gp.reshape(11, 4, 4, ROWS, COLS)
+    gp_m = r.gp.reshape(11 * 768, COLS)
+
+    def weight_piece(p, half):
+        if p == 0:
+            return r.sv.at[:, :, half]
+        if p <= 4:
+            return wa_v.at[half, p - 1]
+        if p <= 8:
+            return w1_v.at[half, p - 5]
+        return w2_v.at[(p - 9) % 2, :, :, half, (p - 9) // 2]
+
+    def grad_piece(p, half):
+        if p == 0:
+            return r.sg.at[:, :, half]
+        if p <= 4:
+            return ga_v.at[half * 4 + p - 1]
+        if p <= 8:
+            return w1_v.at[half, p - 5]
+        return g2_v.at[(p - 9) % 2, :, :, half, (p - 9) // 2]
+
+    def ag_copy(p, i, src, dst, dev):
+        return remote(src, dst, r.ags.at[p, i], r.agr.at[p, i], dev)
+
+    def ag_a(p):
+        v = weight_piece(p, core)
+        for k in (1, 2, 3):
+            ag_copy(p, k - 1, v.at[zpos, xy], v.at[zpos, xy], z_dev(k)).start()
+
+    def ag_b(p):
+        v = weight_piece(p, core)
+        for k in (1, 2, 3):
+            came = v.at[z_of(4 - k), xy]
+            ag_copy(p, k - 1, came, came, z_dev(k)).wait_recv()
+        ag_copy(p, 3, v.at[:, xy], v.at[:, xy], x_dev).start()
+        ag_copy(p, 4, v.at[:, xy], v.at[:, xy], y_dev).start()
+
+    def ag_c(p):
+        v = weight_piece(p, core)
+        ag_copy(p, 3, v.at[:, xy_x], v.at[:, xy_x], x_dev).wait_recv()
+        ag_copy(p, 4, v.at[:, xy_y], v.at[:, xy_y], y_dev).wait_recv()
+        up, down = pl.ds(0, 2), pl.ds(2, 2)
+        ag_copy(p, 5, v.at[down, xy_y], v.at[down, xy_y], x_dev).start()
+        ag_copy(p, 6, v.at[up, xy_x], v.at[up, xy_x], y_dev).start()
+
+    def ag_d(p):
+        v = weight_piece(p, core)
+        up, down = pl.ds(0, 2), pl.ds(2, 2)
+        ag_copy(p, 5, v.at[down, xy_d], v.at[down, xy_d], x_dev).wait_recv()
+        ag_copy(p, 6, v.at[up, xy_d], v.at[up, xy_d], y_dev).wait_recv()
+        ag_copy(p, 7, v, v, sib).start()
+
+    def ag_e(p):
+        v = weight_piece(p, other)
+        ag_copy(p, 7, v, v, sib).wait_recv()
+
+    def ag_f(p):
+        v = weight_piece(p, core)
+        up = pl.ds(0, 2)
+        for k in (1, 2, 3):
+            ag_copy(p, k - 1, v.at[zpos, xy], v.at[zpos, xy], z_dev(k)).wait_send()
+        ag_copy(p, 3, v.at[:, xy], v.at[:, xy], x_dev).wait_send()
+        ag_copy(p, 4, v.at[:, xy], v.at[:, xy], y_dev).wait_send()
+        ag_copy(p, 5, v.at[up, xy_y], v.at[up, xy_y], x_dev).wait_send()
+        ag_copy(p, 6, v.at[up, xy_x], v.at[up, xy_x], y_dev).wait_send()
+        ag_copy(p, 7, v, v, sib).wait_send()
+
+    ahead = 3
+
+    def ag_step(s):
+        if s + ahead <= PIECES:
+            ag_a(s + ahead)
+        if s <= PIECES:
+            ag_b(s)
+        if 1 <= s <= PIECES + 1:
+            ag_c(s - 1)
+        if 2 <= s <= PIECES + 2:
+            ag_d(s - 2)
+
+    order = [9, 10, 11, 12, 5, 6, 7, 8, 4, 1, 2, 3, 0]
+
+    def rs_bufs(n):
+        if n == PIECES:
+            return r.s0, r.s1, r.s2, r.s3
+        q = n % RING
+        return r.l0.at[q], r.l1.at[q], r.l2.at[q], r.l3.at[q]
+
+    def rs_copy(n, i, src, dst, dev):
+        return remote(src, dst, r.rss.at[n, i], r.rsr.at[n, i], dev)
+
+    def credit_wait(n, i):
+        if RING <= n < PIECES:
+            pl.semaphore_wait(r.credit.at[i], 1)
+
+    def credit_give(n, i, dev):
+        if n < PIECES - RING:
+            pl.semaphore_signal(r.credit.at[i], inc=1, device_id=(dev,), device_id_type=MESH_ID)
+
+    def add_into(ref, at, landed):
+        ref[at] = (ref[at].astype(F32) + landed.astype(F32)).astype(ref.dtype)
+
+    def rs_0(n):
+        p = order[n]
+        l0 = rs_bufs(n)[0]
+        credit_wait(n, 0)
+        rs_copy(n, 0, grad_piece(p, other), l0, sib).start()
+
+    def rs_1(n):
+        p = order[n]
+        l0, l1, l2, l3 = rs_bufs(n)
+        g = grad_piece(p, core)
+        rs_copy(n, 0, grad_piece(p, other), l0, sib).wait_recv()
+
+        def body(i, carry):
+            g[i] = (g[i].astype(F32) + l0[i].astype(F32)).astype(g.dtype)
+            return carry
+
+        lax.fori_loop(0, 4, body, 0)
+        credit_give(n, 0, sib)
+        credit_wait(n, 1)
+        rs_copy(n, 1, g.at[pl.ds(2, 2), xy_d], l1.at[0], x_dev).start()
+        credit_wait(n, 2)
+        rs_copy(n, 2, g.at[pl.ds(0, 2), xy_d], l1.at[1], y_dev).start()
+
+    def rs_2(n):
+        p = order[n]
+        l0, l1, l2, l3 = rs_bufs(n)
+        g = grad_piece(p, core)
+        rs_copy(n, 1, g.at[pl.ds(2, 2), xy_d], l1.at[0], x_dev).wait_recv()
+        for i in range(2):
+            g[2 + i, xy_y] = (g[2 + i, xy_y].astype(F32) + l1[0, i].astype(F32)).astype(g.dtype)
+        credit_give(n, 1, x_dev)
+        rs_copy(n, 2, g.at[pl.ds(0, 2), xy_d], l1.at[1], y_dev).wait_recv()
+        for i in range(2):
+            g[i, xy_x] = (g[i, xy_x].astype(F32) + l1[1, i].astype(F32)).astype(g.dtype)
+        credit_give(n, 2, y_dev)
+        credit_wait(n, 3)
+        rs_copy(n, 3, g.at[:, xy_x], l2.at[0], x_dev).start()
+        credit_wait(n, 4)
+        rs_copy(n, 4, g.at[:, xy_y], l2.at[1], y_dev).start()
+
+    def rs_3(n):
+        p = order[n]
+        l0, l1, l2, l3 = rs_bufs(n)
+        g = grad_piece(p, core)
+        rs_copy(n, 3, g.at[:, xy_x], l2.at[0], x_dev).wait_recv()
+        rs_copy(n, 4, g.at[:, xy_y], l2.at[1], y_dev).wait_recv()
+        for i in range(4):
+            g[i, xy] = (
+                g[i, xy].astype(F32) + l2[0, i].astype(F32) + l2[1, i].astype(F32)
+            ).astype(g.dtype)
+        credit_give(n, 3, x_dev)
+        credit_give(n, 4, y_dev)
+        for k in (1, 2, 3):
+            credit_wait(n, 4 + k)
+            rs_copy(n, 4 + k, g.at[z_of(k), xy], l3.at[k - 1], z_dev(k)).start()
+
+    def rs_4(n):
+        p = order[n]
+        l0, l1, l2, l3 = rs_bufs(n)
+        g = grad_piece(p, core)
+        total = g[zpos, xy].astype(F32)
+        for k in (1, 2, 3):
+            rs_copy(n, 4 + k, g.at[z_of(k), xy], l3.at[k - 1], z_dev(k)).wait_recv()
+            total = total + l3[k - 1].astype(F32)
+        for k in (1, 2, 3):
+            credit_give(n, 4 + k, z_dev(4 - k))
+        if p == 0:
+            r.osm[...] = total
+        elif p >= 9:
+            i, j = (p - 9) // 2, (p - 9) % 2
+            r.o2[ROWS * i : ROWS * (i + 1), COLS * j : COLS * (j + 1)] = total
+        else:
+            r.fs[p - 1] = total
+            half = pl.ds(pl.multiple_of(other * 24, 8), 24)
+            rs_copy(n, 8, r.fs.at[p - 1, half], r.fr.at[p - 1], sib).start()
+
+    def rs_5(n):
+        p = order[n]
+        if p == 0 or p >= 9:
+            return
+        half = pl.ds(pl.multiple_of(other * 24, 8), 24)
+        mine = pl.ds(pl.multiple_of(core * 24, 8), 24)
+        rs_copy(n, 8, r.fs.at[p - 1, half], r.fr.at[p - 1], sib).wait_recv()
+        out, first = (r.oq, p - 1) if p <= 3 else ((r.op, 0) if p == 4 else (r.o1, p - 5))
+        for g in range(3):
+            lanes = slice(LANES * g, LANES * (g + 1))
+            base = 768 * first + 256 * g
+            out[:, pl.ds(pl.multiple_of(base + LANES * core, LANES), LANES)] = r.fs[
+                p - 1, mine, lanes
+            ]
+            out[:, pl.ds(pl.multiple_of(base + LANES * other, LANES), LANES)] = r.fr[
+                p - 1, :, lanes
+            ]
+
+    def rs_6(n):
+        p = order[n]
+        l0, l1, l2, l3 = rs_bufs(n)
+        g = grad_piece(p, core)
+        rs_copy(n, 0, grad_piece(p, other), l0, sib).wait_send()
+        rs_copy(n, 1, g.at[pl.ds(2, 2), xy_d], l1.at[0], x_dev).wait_send()
+        rs_copy(n, 2, g.at[pl.ds(0, 2), xy_d], l1.at[1], y_dev).wait_send()
+        rs_copy(n, 3, g.at[:, xy_x], l2.at[0], x_dev).wait_send()
+        rs_copy(n, 4, g.at[:, xy_y], l2.at[1], y_dev).wait_send()
+        for k in (1, 2, 3):
+            rs_copy(n, 4 + k, g.at[z_of(k), xy], l3.at[k - 1], z_dev(k)).wait_send()
+        if 1 <= p <= 8:
+            half = pl.ds(pl.multiple_of(other * 24, 8), 24)
+            rs_copy(n, 8, r.fs.at[p - 1, half], r.fr.at[p - 1], sib).wait_send()
+
+    rs_stages = (rs_0, rs_1, rs_2, rs_3, rs_4, rs_5, rs_6)
+
+    base = [0, 1, 2, 3, 6, 7, 8, 9, 10, 14, 15, 16, 18]
+
+    def rs_step(s):
+        for i, stage in enumerate(rs_stages):
+            if s - i in base:
+                stage(base.index(s - i))
+
+    def rows_of(f):
+        return pl.ds(pl.multiple_of(f * WIN, WIN), WIN)
+
+    def loop(count, body, ticks=()):
+        def step(i, carry):
+            body(i)
+            for k, tick in enumerate(ticks):
+                if tick is not None:
+                    pl.when(i == k)(tick)
+            return carry
+
+        lax.fori_loop(0, count, step, 0)
+
+    def steps(fn, *numbers):
+        return [functools.partial(fn, s) if s is not None else None for s in numbers]
+
+    def natural(ref, lead, rows):
+        parts = []
+        for g in range(3):
+            for h in range(2):
+                parts.append(ref[(h, *lead, rows, pl.ds(LANES * g, LANES))])
+        return parts
+
+    def put(ref, lead, rows, value):
+        for g in range(3):
+            for h in range(2):
+                at = 256 * g + LANES * h
+                ref[(h, *lead, rows, pl.ds(LANES * g, LANES))] = value[:, at : at + LANES]
+
+    def put_a(piece, rows, value):
+        for g in range(3):
+            for h in range(2):
+                at = 256 * g + LANES * h
+                r.gp[4 * h + piece, rows, LANES * g : LANES * (g + 1)] = value[:, at : at + LANES]
+
+    def pre_rows(t, h, s):
+        return pl.ds(pl.multiple_of((2 * t + h) * 1024 + s.start, 8), s.stop - s.start)
+
+    def pre_tile(t, s):
+        return jnp.concatenate([gp_m[pre_rows(t, h, s), :] for h in range(2)], axis=1)
+
+    def mixed_in(f):
+        rw = rows_of(f)
+        return jnp.where(r.st[rw, 0:1] > 0, r.v24[6:7, :], r.tok[rw, :].astype(F32))
+
+    def masks():
+        bits = jnp.transpose(r.mask[...].astype(F32))
+        for j in range(8):
+            keep = 1.0 - r.pad[j // 2].astype(F32)
+            col = bits[:, j : j + 1]
+            r.st[LANES * j : LANES * (j + 1), 0:1] = col
+            r.st[LANES * j : LANES * (j + 1), 1:2] = col * keep
+
+    def mask_grad(f):
+        rw = rows_of(f)
+        r.dm[rw, :] = (r.dm[rw, :].astype(F32) * r.st[rw, 1:2]).astype(BF16)
+
+    def spread_small():
+        table = r.sv[...].reshape(32, 16, LANES).astype(F32)
+        rows = [table[:, i, :].astype(BF16) for i in range(3)]
+        at = 0
+        for name, row, lane0, width in SMALL_ROWS:
+            pick, owner = spread_tables(lane0, width)
+            full = jnp.sum(jnp.where(owner, dot_nn(rows[row], pick), 0.0), axis=0, keepdims=True)
+            if name == "qkv_bias":
+                r.bqkv[...] = full
+            elif name == "fc1_bias":
+                r.bfc1[...] = full
+            else:
+                r.v24[at : at + 1, :] = full
+                at += 1
+        r.gv[...] = jnp.zeros_like(r.gv)
+
+    def collect_small():
+        table = [jnp.zeros((32, LANES), F32) for _ in range(3)]
+        at = 0
+        for name, row, lane0, width in SMALL_ROWS:
+            pick, owner = spread_tables(lane0, width)
+            if name == "qkv_bias":
+                full = r.gbqkv[...]
+            elif name == "fc1_bias":
+                full = r.gbfc1[...]
+            else:
+                full = r.gv[at : at + 1, :]
+                at += 1
+            parts = jnp.where(owner, full, 0.0)
+            for _ in range(3):
+                high = parts.astype(BF16)
+                table[row] = table[row] + dot_nt(high, pick)
+                parts = parts - high.astype(F32)
+        flat = r.sg.reshape(256, LANES)
+        r.sg[...] = jnp.zeros_like(r.sg)
+        for i in range(3):
+            flat[pl.ds(i, 32, stride=8), :] = table[i]
+
+    def ln1(f):
+        rw = rows_of(f)
+        x = mixed_in(f)
+        row_mean, row_scale = row_stats(x)
+        r.st[rw, 2:3] = row_mean
+        r.st[rw, 3:4] = row_scale
+        r.normed[rw, :] = ((x - row_mean) * row_scale * r.v24[0:1, :] + r.v24[1:2, :]).astype(BF16)
+
+    def qkv(t):
+        w = jnp.concatenate(natural(wa_m, (t,), pl.ds(0, 768)), axis=1)
+        cols = slice(768 * t, 768 * (t + 1))
+        bias = r.bqkv[:, cols]
+        for i in range(4):
+            s = slice(WIN * i, WIN * (i + 1))
+            r.packed[s, cols] = (dot_nn(r.normed[s, :], w) + bias).astype(BF16)
+
+    low_lanes = lax.broadcasted_iota(jnp.int32, (WIN, LANES), 1) < HEAD_DIM
+
+    def two_heads(a):
+        z = jnp.zeros_like(a)
+        return jnp.concatenate([jnp.where(low_lanes, a, z), jnp.where(low_lanes, z, a)], axis=0)
+
+    def attention(f):
+        rw = rows_of(f)
+        for hp in range(HEADS // 2):
+            part = lambda i: slice(768 * i + LANES * hp, 768 * i + LANES * (hp + 1))
+            q2 = r.packed[rw, part(0)] * jnp.asarray(0.125, BF16)
+            k2 = r.packed[rw, part(1)]
+            v2 = r.packed[rw, part(2)]
+            scores = dot_nt(two_heads(q2), k2)
+            row_max = jnp.max(scores, axis=1, keepdims=True)
+            e = jnp.exp(scores - row_max)
+            total = jnp.sum(e, axis=1, keepdims=True)
+            inv = 1.0 / total
+            log_total = row_max + jnp.log(total)
+            for h in range(2):
+                col = jnp.broadcast_to(log_total[WIN * h : WIN * (h + 1)], (WIN, 8))
+                r.lse[f * 6 + hp, h : h + 1, :] = jnp.transpose(col)[0:1]
+            e = e.astype(BF16)
+            out = dot_nn(jnp.concatenate([e[:WIN], e[WIN:]], axis=1), two_heads(v2))
+            scale = jnp.where(
+                low_lanes,
+                jnp.broadcast_to(inv[:WIN], (WIN, LANES)),
+                jnp.broadcast_to(inv[WIN:], (WIN, LANES)),
+            )
+            r.att[rw, part(0)] = (out * scale).astype(BF16)
+
+    def project(f):
+        rw = rows_of(f)
+        w = jnp.concatenate(natural(wa_m, (3,), pl.ds(0, 768)), axis=1)
+        middle = mixed_in(f) + (dot_nn(r.att[rw, :], w) + r.v24[2:3, :])
+        r.mid[rw, :] = middle
+        row_mean, row_scale = row_stats(middle)
+        r.st[rw, 4:5] = row_mean
+        r.st[rw, 5:6] = row_scale
+        r.n2[rw, :] = ((middle - row_mean) * row_scale * r.v24[3:4, :] + r.v24[4:5, :]).astype(BF16)
+
+    def tile(t):
+        return pl.ds(pl.multiple_of(t * 768, 768), 768)
+
+    def fc1(t):
+        w = jnp.concatenate(natural(w1_m, (t,), pl.ds(0, 768)), axis=1)
+        cols = tile(t)
+        bias = r.bfc1[:, cols]
+        for i in range(4):
+            s = slice(WIN * i, WIN * (i + 1))
+            act, slope = gelu_and_slope(dot_nn(r.n2[s, :], w) + bias)
+            r.hact[s, cols] = act.astype(BF16)
+            slope = slope.astype(BF16)
+            gp_m[pre_rows(t, 0, s), :] = slope[:, :COLS]
+            gp_m[pre_rows(t, 1, s), :] = slope[:, COLS:]
+
+    def turn(src):
+        def body(f):
+            rw = rows_of(f)
+            r.tr[:, rw] = r.normed[rw, :].T if src == 0 else r.n2[rw, :].T
+
+        return body
+
+    def fc2(n):
+        cols = pl.ds(pl.multiple_of(n * 256, 256), 256)
+        parts = []
+        for i in range(2):
+            g = 2 * n + i
+            lanes = pl.ds(pl.multiple_of(lax.rem(g, 3) * LANES, LANES), LANES)
+            parts.append(w2_m[lax.div(g, 3), :, lanes])
+        w = jnp.concatenate(parts, axis=1)
+        for i in range(4):
+            s = slice(WIN * i, WIN * (i + 1))
+            r.n2[s, cols] = (
+                dot_nn(r.hact[s, :], w) + (r.mid[s, cols] + r.v24[5:6, cols])
+            ).astype(BF16)
+
+    def grad_fc2(t):
+        cols = tile(t)
+        g = dot_tn(r.hact[:, cols], r.dm[...]).astype(BF16)
+        g2_m[0, cols, :] = g[:, :COLS]
+        g2_m[1, cols, :] = g[:, COLS:]
+
+    def grad_pre(t):
+        cols = tile(t)
+        w = jnp.concatenate([w2_m[0, cols, :], w2_m[1, cols, :]], axis=1)
+        sums = jnp.zeros((1, 768), F32)
+        for i in range(4):
+            s = slice(WIN * i, WIN * (i + 1))
+            d = (dot_nt(r.dm[s, :], w) * pre_tile(t, s).astype(F32)).astype(BF16)
+            gp_m[pre_rows(t, 0, s), :] = d[:, :COLS]
+            gp_m[pre_rows(t, 1, s), :] = d[:, COLS:]
+            sums = sums + jnp.sum(d.astype(F32), axis=0, keepdims=True)
+        r.gbfc1[:, cols] = sums
+
+    def grad_fc1(t):
+        put(w1_m, (t,), pl.ds(0, 768), dot_nn(r.tr[...], pre_tile(t, slice(0, 1024))).astype(BF16))
+
+    def grad_norm_two(n):
+        rw = rows_of(n)
+        parts = []
+        for t in range(4):
+            parts += natural(w1_m, (t,), rw)
+        w = jnp.concatenate(parts, axis=1)
+        for i in range(4):
+            s = slice(WIN * i, WIN * (i + 1))
+            pre = jnp.concatenate([pre_tile(t, s) for t in range(4)], axis=1)
+            r.dn[s, rw] = dot_nt(pre, w)
+
+    def grad_middle(f):
+        rw = rows_of(f)
+        dy = r.dm[rw, :].astype(F32)
+        dx, gain, shift = norm_backward(
+            r.mid[rw, :], r.st[rw, 4:5], r.st[rw, 5:6], r.dn[rw, :], r.v24[3:4, :]
+        )
+        d = dy + dx
+        low = d.astype(BF16)
+        r.mid[rw, :] = d
+        r.dm[rw, :] = low
+        r.gv[3:4, :] += gain
+        r.gv[4:5, :] += shift
+        r.gv[5:6, :] += jnp.sum(dy, axis=0, keepdims=True)
+        r.gv[2:3, :] += jnp.sum(low.astype(F32), axis=0, keepdims=True)
+
+    def grad_proj(j):
+        rw = rows_of(j)
+        put_a(3, rw, dot_tn(r.att[:, rw], r.dm[...]).astype(BF16))
+
+    def grad_att(f):
+        rw = rows_of(f)
+        w = jnp.concatenate(natural(wa_m, (3,), pl.ds(0, 768)), axis=1)
+        r.n2[rw, :] = dot_nt(r.dm[rw, :], w).astype(BF16)
+
+    def attention_backward(f):
+        rw = rows_of(f)
+        for hp in range(HEADS // 2):
+            part = lambda i: slice(768 * i + LANES * hp, 768 * i + LANES * (hp + 1))
+            q2 = r.packed[rw, part(0)] * jnp.asarray(0.125, BF16)
+            k2 = r.packed[rw, part(1)]
+            v2 = r.packed[rw, part(2)]
+            qs, ds, ks = two_heads(q2), two_heads(r.n2[rw, part(0)]), two_heads(k2)
+            log_total = jnp.concatenate(
+                [r.lse[f * 6 + hp, 0:1, :], r.lse[f * 6 + hp, 1:2, :]], axis=1
+            )
+            probs = jnp.exp(dot_nt(k2, qs) - log_total)
+            prod = probs * dot_nt(v2, ds)
+            row_dot = jnp.sum(prod, axis=0, keepdims=True)
+            d_scores = (prod - probs * row_dot).astype(BF16)
+            r.packed[rw, part(2)] = dot_nn(probs.astype(BF16), ds).astype(BF16)
+            r.packed[rw, part(1)] = dot_nn(d_scores, qs).astype(BF16)
+            stacked = jnp.concatenate([d_scores[:, :WIN], d_scores[:, WIN:]], axis=0)
+            r.packed[rw, part(0)] = (dot_tn(stacked, ks) * 0.125).astype(BF16)
+
+    def grad_qkv(t):
+        cols = slice(768 * t, 768 * (t + 1))
+        d = r.packed[:, cols]
+        put_a(t, slice(None), dot_nn(r.tr[...], d).astype(BF16))
+        r.gbqkv[:, cols] = jnp.sum(d.astype(F32), axis=0, keepdims=True)
+
+    def grad_norm_one(n):
+        rw = rows_of(n)
+        parts = []
+        for t in range(3):
+            parts += natural(wa_m, (t,), rw)
+        w = jnp.concatenate(parts, axis=1)
+        for i in range(4):
+            s = slice(WIN * i, WIN * (i + 1))
+            r.dn[s, rw] = dot_nt(r.packed[s, :], w)
+
+    def grad_mixed(f):
+        rw = rows_of(f)
+        dx, gain, shift = norm_backward(
+            mixed_in(f), r.st[rw, 2:3], r.st[rw, 3:4], r.dn[rw, :], r.v24[0:1, :]
+        )
+        d = r.mid[rw, :] + dx
+        chosen = r.st[rw, 0:1] > 0
+        r.dn[rw, :] = jnp.where(chosen, 0.0, d)
+        r.gv[0:1, :] += gain
+        r.gv[1:2, :] += shift
+        r.gv[6:7, :] += jnp.sum(jnp.where(chosen, d, 0.0), axis=0, keepdims=True)
+
+    loads = [
+        pltpu.make_async_copy(r.og_in, r.dm, r.ld.at[0]),
+        pltpu.make_async_copy(r.tok_in, r.tok, r.ld.at[1]),
+    ]
+    for q in range(2):
+        loads.append(
+            pltpu.make_async_copy(
+                r.s2w.at[:, pl.ds(COLS * q, COLS)], w2_shard.at[q, zpos, xy, core], r.ld.at[2 + q]
+            )
+        )
+    loads.append(pltpu.make_async_copy(r.small, r.sv.at[zpos, xy, core], r.ld.at[4]))
+    for copy in loads:
+        copy.start()
+
+    barrier = pltpu.get_barrier_semaphore()
+    peers = [sib, x_dev, y_dev, z_dev(1), z_dev(2), z_dev(3)]
+    for dev in peers:
+        pl.semaphore_signal(barrier, inc=1, device_id=(dev,), device_id_type=MESH_ID)
+
+    def shard_half(t, half):
+        ref, first = (r.sq, t) if t < 3 else ((r.sp, 0) if t == 3 else (r.s1w, t - 4))
+        parts = []
+        for g in range(3):
+            base = 768 * first + 256 * g
+            a = ref[:, base : base + LANES].astype(F32)
+            b = ref[:, base + LANES : base + 2 * LANES].astype(F32)
+            parts.append(jnp.where(half == 0, a, b))
+        return jnp.concatenate(parts, axis=1)
+
+    for t in range(8):
+        away = jnp.concatenate([shard_half(t, other), jnp.zeros((8, COLS), F32)], axis=0)
+        r.tx[t] = away.astype(BF16)
+    pl.semaphore_wait(barrier, len(peers))
+    swap = remote(r.tx, r.rx, r.prep.at[0], r.prep.at[1], sib)
+    swap.start()
+    loads[4].wait()
+    ag_a(0)
+    swap.wait()
+    for t in range(8):
+        here = shard_half(t, core)
+        there = r.rx[t].astype(F32)[:24]
+        block = jnp.concatenate(
+            [jnp.where(core == 0, here, there), jnp.where(core == 0, there, here)], axis=0
+        ).astype(BF16)
+        if t < 4:
+            wa_v[core, t, zpos, xy] = block
+        else:
+            w1_v[core, t - 4, zpos, xy] = block
+    for p in range(1, ahead):
+        ag_a(p)
+    loads[2].wait()
+    loads[3].wait()
+    ag_step(0)
+    masks()
+    ag_step(1)
+    loads[0].wait()
+    loop(4, mask_grad)
+    ag_step(2)
+    ag_e(0)
+    loads[1].wait()
+    spread_small()
+    ag_step(3)
+    loop(4, ln1)
+    ag_e(1)
+    qkv(0)
+    ag_step(4)
+    ag_e(2)
+    qkv(1)
+    ag_step(5)
+    ag_e(3)
+    qkv(2)
+    ag_step(6)
+    loop(4, attention, steps(ag_step, None, 7, 8, 9))
+    ag_e(4)
+    loop(4, project)
+    keep_middle = pltpu.make_async_copy(r.mid, r.ig, r.ld.at[5])
+    keep_middle.start()
+
+    def arrive(p, s=None):
+        def go():
+            if s is not None:
+                ag_step(s)
+            ag_e(p)
+
+        return go
+
+    arrive(5)()
+    loop(4, fc1, [arrive(6, 10), arrive(7, 11), arrive(8), functools.partial(ag_step, 12)])
+    loop(4, turn(1))
+    loop(4, grad_fc2, steps(ag_step, None, 13, None, 14))
+    rs_step(0)
+    for p in range(PIECES + 1):
+        if p >= 9:
+            ag_e(p)
+        ag_f(p)
+    rs_step(1)
+    loop(4, grad_pre, steps(rs_step, None, 2, None, 3))
+    loop(3, grad_norm_two, steps(rs_step, 4, None, 5))
+    loop(4, grad_fc1, steps(rs_step, 6, None, None, 7))
+    keep_middle.wait()
+    loop(4, grad_middle)
+    rs_step(8)
+    loop(3, grad_proj)
+    loop(4, grad_att)
+    rs_step(9)
+    loop(4, attention_backward, steps(rs_step, 10, 11, 12, 13))
+    loop(4, turn(0))
+    for t in range(3):
+        grad_qkv(t)
+        rs_step(14 + t)
+    loop(3, grad_norm_one, steps(rs_step, None, 17, None))
+    loop(4, grad_mixed)
+    collect_small()
+    load_middle = pltpu.make_async_copy(r.ig, r.mid, r.ld.at[6])
+    load_middle.start()
+    rs_step(18)
+    load_middle.wait()
+    write_grad = pltpu.make_async_copy(r.dn, r.ig, r.ld.at[7])
+    write_grad.start()
+    loop(3, fc2, steps(rs_step, 19, 20, None))
+    write_out = pltpu.make_async_copy(r.n2, r.bo, r.ld.at[0])
+    write_out.start()
+    rs_step(21)
+    rs_step(22)
+    rs_step(23)
+    rs_step(24)
+    write_grad.wait()
+    write_out.wait()
+
+
+def fused_device(
+    tokens,
+    mask_bits,
+    pad_flags,
+    ln1_gain,
+    ln1_bias,
+    qkv_weight,
+    qkv_bias,
+    proj_weight,
+    proj_bias,
+    ln2_gain,
+    ln2_bias,
+    fc1_weight,
+    fc1_bias,
+    fc2_weight,
+    fc2_bias,
+    mask_embed,
+    out_grad,
+):
+    pad = jnp.zeros((8,), BF16)
+    small = jnp.concatenate(
+        [ln1_gain, ln1_bias, proj_bias, ln2_gain, ln2_bias, pad, fc2_bias, mask_embed, qkv_bias]
+        + [pad, fc1_bias, jnp.zeros((32 + 13 * LANES,), BF16)]
+    ).reshape(16, LANES)
+    any_spec = pl.BlockSpec(memory_space=pl.ANY)
+    vmem = pl.BlockSpec(memory_space=pltpu.VMEM)
+    smem = pl.BlockSpec(memory_space=pltpu.SMEM)
+    shape = jax.ShapeDtypeStruct
+    outs = pl.pallas_call(
+        fused_kernel,
+        out_shape=(
+            shape((1024, 768), BF16),
+            shape((1024, 768), F32),
+            shape((24, 2304), F32),
+            shape((24, 768), F32),
+            shape((24, 3072), F32),
+            shape((96, 768), F32),
+            shape((8, LANES), F32),
+        ),
+        in_specs=[any_spec, any_spec, vmem, smem, any_spec, vmem, vmem, vmem, any_spec],
+        out_specs=(any_spec, any_spec, vmem, vmem, vmem, vmem, vmem),
+        scratch_shapes=[pltpu.VMEM(*spec) for spec in SCRATCH.values()] + list(SEMS.values()),
+        compiler_params=pltpu.CompilerParams(
+            collective_id=0, has_side_effects=True, vmem_limit_bytes=64 * 2**20
+        ),
+    )(
+        tokens,
+        out_grad,
+        mask_bits.reshape(8, LANES),
+        pad_flags,
+        small,
+        qkv_weight,
+        proj_weight,
+        fc1_weight,
+        fc2_weight,
+    )
+    block_out, input_grad, gq, gpj, g1, g2, gsmall = outs
+    v = {name: gsmall[row, lane : lane + width] for name, row, lane, width in SMALL_ROWS}
+    return (
+        block_out,
+        input_grad,
+        v["ln1_gain"],
+        v["ln1_bias"],
+        gq,
+        v["qkv_bias"],
+        gpj,
+        v["proj_bias"],
+        v["ln2_gain"],
+        v["ln2_bias"],
+        g1,
+        v["fc1_bias"],
+        g2,
+        v["fc2_bias"],
+        v["mask_embed"],
+    )
+
+
 def solution(mesh):
     placed = (
         P("fsdp", None),
@@ -329,7 +1218,7 @@
         P("fsdp", None),
     )
     return jax.shard_map(
-        per_device,
+        fused_device if mesh.shape["fsdp"] == 32 else per_device,
         mesh=mesh,
         in_specs=placed,
         out_specs=(

time: 831 us -> 202 us (0.24); the launches traced: 820 us -> 202 us
  waiting for transfers between devices: 474 us -> 0 us
  Pallas kernels: 0 us -> 183 us
  matrix products: 144 us -> 0 us
  blocking collectives: 83.9 us -> 0 us
  local copies, waits for them, and re-layouts: 74.8 us -> 17.9 us
  other arithmetic: 28.7 us -> 0 us
  between operations: 15 us -> 0.69 us
    reduce_scatter x4 -> x0, waiting for transfers between devices: 361 us -> none  [the longest x1 142 us: per_device(): lax.psum_scatter(mlp_grads[4], 'fsdp', scatter_dimension=0, tiled=True)]
    pallas_call x0 -> x1, Pallas kernels: none -> 183 us  [fused_device(): pl.pallas_call(fused_kernel, out_shape=(shape((1024, 768), BF16), shape((...]
    dot_general x18 -> x0, matrix products: 144 us -> none  [the longest x1 37.7 us: forward_pass(): jnp.dot(normed_two, up_w, preferred_element_type=jnp.float32)]
    all_gather x4 -> x0, waiting for transfers between devices: 109 us -> none  [the longest x1 59.9 us: per_device(): lax.all_gather(fc1_weight, 'fsdp', axis=0, tiled=True)]
    unnamed x2 -> x0, blocking collectives: 83.9 us -> none
    unnamed x115 -> x16, local copies, waits for them, and re-layouts: 37.3 us -> 7.23 us
    reduce_sum x11 -> x0, other arithmetic: 17.8 us -> none  [the longest x2 5.66 us: norm_rows(): return centered * lax.rsqrt(variance + epsilon) * gain_vec + shift_vec]
    convert_element_type x4 -> x0, local copies, waits for them, and re-layouts: 14.2 us -> none  [the longest x1 6.66 us: forward_pass(): packed = (jnp.dot(normed, qkv_w, preferred_element_type=jnp.float32) + qk...]
  transfers between devices with their start and end apart: 8 -> 0, of which waited for: 7 -> 0; matrix products, arithmetic and copies ran while one was open for 23% -> 0% of each run, Pallas kernels for 0% -> 0%
where the time goes in v1:
time: 202 us
  Pallas kernels  183 us (91%)
  local copies, waits for them, and re-layouts  17.9 us (9%)
    pallas_call x1, Pallas kernels, fused_device(): pl.pallas_call(fused_kernel, out_shape=(shape((1024, 768), BF16), shape((...  183 us
    unnamed x16, local copies, waits for them, and re-layouts  7.23 us
    concatenate x1, local copies, waits for them, and re-layouts, fused_device(): jnp.concatenate([ln1_gain, ln1_bias, proj_bias, ln2_gain, ln2_bias, pad,...  6.69 us

profile of v1, /device:TPU:0, one launch (start us, length us, event | category | flops | bytes accessed | tf_op | source)
XLA Modules:
  0.0 202.1 jit_solution(4425251606383772940)
XLA Ops:
  0.7 6.7 %concatenate.3 = bf16[2048]{0:T(1024)(128)(2,1)} concatenate(bf16[24]{0:T(256)(128)(2,1)} %param.20, bf16[24]{0:T(256)(128)(2,1)} %param.21, bf16[24]{0:T(256)(128)(2,1)} %param.25, bf16[24]{0:T(256)(128)(2,1)} %param.26, bf16[24]{0:T(256)(128)(2,1)} %param.27, bf16[8]{0:T(256)(128)(2,1)S(1)} %broadcast.3, bf16[24]{0:T(256)(128)(2,1)} %param.31, bf16[24]{0:T(256)(128)(2,1)} %param.32, ...), dimensions={0} | concatenate | bytes 8192 | tf_op jit(solution)/shard_map/concatenate | solution.py:1143
  7.4 183.4 %shard_map.280 = (bf16[1024,768]{1,0:T(8,128)(2,1)}, f32[1024,768]{1,0:T(8,128)}, f32[24,2304]{1,0:T(8,128)}, f32[24,768]{1,0:T(8,128)}, f32[24,3072]{1,0:T(8,12...) custom-call(bf16[1024,768]{1,0:T(8,128)(2,1)} %refs_0_.1, bf16[1024,768]{1,0:T(8,128)(2,1)} %refs_1_.1, s32[8,128]{1,0:T(8,128)} %bitcast.21, ...), custom_call_target="tpu_custom_call" | custom-call | tf_op jit(solution)/shard_map/pallas_call | solution.py:1151
  190.8 1.5 slice_bitcast_fusion
  192.4 1.3 slice_bitcast_fusion.6
  193.6 1.2 slice_bitcast_fusion.2
  194.8 0.0 copy-start
  194.8 2.8 %copy.38 = bf16[1024,768]{1,0:T(8,128)(2,1)} copy(bf16[1024,768]{1,0:T(8,128)(2,1)} %get-tuple-element.51) | data formatting | bytes 3145728
  197.6 0.0 copy-done
  197.6 0.0 copy-start.3
  197.6 0.0 copy-start.4
  197.6 0.0 copy-start.2
  197.6 0.0 copy-start.1
  197.6 1.7 copy.39
  199.3 0.0 copy-done.3
  199.3 0.7 copy.40
  200.0 0.0 copy-done.4
  200.0 0.6 copy.41
  200.6 0.0 copy-done.2
  200.6 0.7 copy.42
  201.3 0.0 copy-done.1
  201.3 0.7 copy.43
  (2 shorter events, 0.0 us)
Async XLA Ops:
  194.8 2.8 %copy-start = (f32[1024,768]{1,0:T(8,128)S(1)}, f32[1024,768]{1,0:T(8,128)}, u32[]{:S(2)}) copy-start(f32[1024,768]{1,0:T(8,128)} %get-tuple-element.52) | copy-start | bytes 9437188
  197.6 1.7 copy-start.3
  197.6 2.4 %copy-start.4 = (f32[24,768]{1,0:T(8,128)S(1)}, f32[24,768]{1,0:T(8,128)}, u32[]{:S(2)}) copy-start(f32[24,768]{1,0:T(8,128)} %get-tuple-element.57) | copy-start | bytes 221188
  197.6 3.0 %copy-start.2 = (f32[24,3072]{1,0:T(8,128)S(1)}, f32[24,3072]{1,0:T(8,128)}, u32[]{:S(2)}) copy-start(f32[24,3072]{1,0:T(8,128)} %get-tuple-element.61) | copy-start | bytes 884740
  197.6 3.7 %copy-start.1 = (f32[96,768]{1,0:T(8,128)S(1)}, f32[96,768]{1,0:T(8,128)}, u32[]{:S(2)}) copy-start(f32[96,768]{1,0:T(8,128)} %get-tuple-element.63) | copy-start | bytes 884740

commit v2 on v1

--- a/solution.py
+++ b/solution.py
@@ -318,7 +318,10 @@
 ROWS = 48
 COLS = 384
 PIECES = 12
-RING = 4
+CUT = 16
+RINGS = dict(l0=2, l1=4, lz=4, lt=4, l2=4, l3=4)
+CREDIT_RINGS = ["l0", "l1", "lt", "l2", "l2"] + ["lz"] * 4 + ["l3"] * 4
+SHORT = 11
 MESH_ID = pl.DeviceIdType.MESH
 
 
@@ -401,29 +404,31 @@
     w1=((8, 768, COLS), BF16),
     w2=((8, 768, COLS), BF16),
     g2=((8, 768, COLS), BF16),
-    sv=((4, 4, 2, 16, LANES), BF16),
+    sv=((4, 4, 2, 8, LANES), F32),
     sg=((4, 4, 2, 8, LANES), F32),
-    tx=((8, 32, COLS), BF16),
-    rx=((8, 32, COLS), BF16),
     fs=((8, ROWS, COLS), F32),
     fr=((8, ROWS // 2, COLS), F32),
-    l0=((RING, 4, 4, ROWS, COLS), BF16),
-    l1=((RING, 2, 2, ROWS, COLS), BF16),
-    l2=((RING, 2, 4, ROWS, COLS), BF16),
-    l3=((RING, 3, ROWS, COLS), BF16),
+    l0=((RINGS["l0"], 4, 4, ROWS, COLS), BF16),
+    l1=((RINGS["l1"], 4, CUT, COLS), BF16),
+    lz=((RINGS["lz"], 4, ROWS - CUT, COLS), BF16),
+    lt=((RINGS["lt"], ROWS - CUT, COLS), BF16),
+    l2=((RINGS["l2"], 2, 4, ROWS, COLS), BF16),
+    l3=((RINGS["l3"], 4, ROWS, COLS), BF16),
+    l1s=((4, ROWS, COLS), BF16),
+    l3s=((4, ROWS, COLS), BF16),
     s0=((4, 4, 8, LANES), F32),
-    s1=((2, 2, 8, LANES), F32),
+    s1=((4, 8, LANES), F32),
     s2=((2, 4, 8, LANES), F32),
-    s3=((3, 8, LANES), F32),
+    s3=((4, 8, LANES), F32),
 )
 SEMS = dict(
     ld=pltpu.SemaphoreType.DMA((8,)),
     prep=pltpu.SemaphoreType.DMA((2,)),
-    ags=pltpu.SemaphoreType.DMA((PIECES + 1, 8)),
-    agr=pltpu.SemaphoreType.DMA((PIECES + 1, 8)),
-    rss=pltpu.SemaphoreType.DMA((PIECES + 1, 9)),
-    rsr=pltpu.SemaphoreType.DMA((PIECES + 1, 9)),
-    credit=pltpu.SemaphoreType.REGULAR((8,)),
+    ags=pltpu.SemaphoreType.DMA((PIECES + 1, 17)),
+    agr=pltpu.SemaphoreType.DMA((PIECES + 1, 17)),
+    rss=pltpu.SemaphoreType.DMA((PIECES + 1, 19)),
+    rsr=pltpu.SemaphoreType.DMA((PIECES + 1, 19)),
+    credit=pltpu.SemaphoreType.REGULAR((32,)),
 )
 
 
@@ -503,92 +508,296 @@
     def ag_copy(p, i, src, dst, dev):
         return remote(src, dst, r.ags.at[p, i], r.agr.at[p, i], dev)
 
+    def rows_one(p):
+        return pl.ds(0, CUT) if p else pl.ds(0, 8)
+
+    def rs_rows_one(n):
+        return pl.ds(0, ROWS) if SHORT <= n < PIECES else rows_one(order[n])
+
+    rows_two = pl.ds(CUT, ROWS - CUT)
+
+    def sides(p):
+        along_x, along_y = (x_dev, xy_x), (y_dev, xy_y)
+        return (along_x, along_y) if p % 2 == 0 else (along_y, along_x)
+
+    at_start, at_end = zpos == 0, zpos == 3
+    inside = jnp.logical_and(zpos > 0, zpos < 3)
+
+    def along_z(fn):
+        pl.when(jnp.logical_not(at_end))(lambda: fn(1))
+        fn(2)
+        pl.when(jnp.logical_not(at_start))(lambda: fn(3))
+
+    def pass_to_end(fn):
+        pl.when(zpos == 1)(lambda: fn(3, 3))
+        pl.when(zpos == 2)(lambda: fn(0, 1))
+
+    def ag_z(p, k, at):
+        return ag_copy(p, k - 1, at, at, z_dev(k))
+
+    def ag_z2(p, k, at):
+        return ag_copy(p, 12 + k, at, at, z_dev(k))
+
+    def ag_z_from(p, k, at, base=0):
+        return ag_copy(p, base + k - 1, at, at, z_dev(k))
+
+    def ag_pass(p, far, k, at, base=0):
+        return ag_copy(p, base + (0 if k == 3 else 2), at, at, z_dev(k))
+
+    def ag_x(p, k, v):
+        at = v.at[z_of(4 - k), xy] if k else v.at[zpos, xy]
+        return ag_copy(p, 3 + k, at, at, x_dev)
+
+    def ag_y(p, k, v):
+        at = v.at[z_of(4 - k), xy] if k else v.at[zpos, xy]
+        return ag_copy(p, 7 + k, at, at, y_dev)
+
+    def from_x(p, k, v):
+        at = v.at[z_of(4 - k), xy_x] if k else v.at[zpos, xy_x]
+        return ag_copy(p, 3 + k, at, at, x_dev)
+
+    def from_y(p, k, v):
+        at = v.at[z_of(4 - k), xy_y] if k else v.at[zpos, xy_y]
+        return ag_copy(p, 7 + k, at, at, y_dev)
+
+    def from_a(p, k, v):
+        return from_x(p, k, v) if p % 2 == 0 else from_y(p, k, v)
+
+    def from_b(p, k, v):
+        return from_y(p, k, v) if p % 2 == 0 else from_x(p, k, v)
+
+    def ag_one(p, v, col):
+        at = v.at[:, col, rows_one(p)]
+        return ag_copy(p, 11, at, at, sides(p)[1][0])
+
+    def ag_two(p, v, col):
+        at = v.at[zpos, col, rows_two]
+        return ag_copy(p, 12, at, at, sides(p)[0][0])
+
     def ag_a(p):
         v = weight_piece(p, core)
-        for k in (1, 2, 3):
-            ag_copy(p, k - 1, v.at[zpos, xy], v.at[zpos, xy], z_dev(k)).start()
+        along_z(lambda k: ag_z(p, k, v.at[zpos, xy]).start())
+        ag_x(p, 0, v).start()
+        ag_y(p, 0, v).start()
 
     def ag_b(p):
         v = weight_piece(p, core)
-        for k in (1, 2, 3):
-            came = v.at[z_of(4 - k), xy]
-            ag_copy(p, k - 1, came, came, z_dev(k)).wait_recv()
-        ag_copy(p, 3, v.at[:, xy], v.at[:, xy], x_dev).start()
-        ag_copy(p, 4, v.at[:, xy], v.at[:, xy], y_dev).start()
-
-    def ag_c(p):
+        for k in (1, 3):
+            ag_z_from(p, k, v.at[z_of(4 - k), xy]).wait_recv()
+            ag_x(p, k, v).start()
+            ag_y(p, k, v).start()
+
+    def ag_b2(p):
         v = weight_piece(p, core)
-        ag_copy(p, 3, v.at[:, xy_x], v.at[:, xy_x], x_dev).wait_recv()
-        ag_copy(p, 4, v.at[:, xy_y], v.at[:, xy_y], y_dev).wait_recv()
-        up, down = pl.ds(0, 2), pl.ds(2, 2)
-        ag_copy(p, 5, v.at[down, xy_y], v.at[down, xy_y], x_dev).start()
-        ag_copy(p, 6, v.at[up, xy_x], v.at[up, xy_x], y_dev).start()
+        ag_z_from(p, 2, v.at[z_of(2), xy]).wait_recv()
+        pass_to_end(lambda far, k: ag_pass(p, far, k, v.at[far, xy]).start())
+        ag_x(p, 2, v).start()
+        ag_y(p, 2, v).start()
+
+    def ag_c2(p):
+        if p:
+            v = weight_piece(p, core)
+            from_b(p, 0, v).wait_recv()
+            ag_two(p, v, sides(p)[1][1]).start()
+
+    def ag_c3(p):
+        if p:
+            v = weight_piece(p, core)
+            ag_two(p, v, xy_d).wait_recv()
+            along_z(lambda k: ag_z2(p, k, v.at[zpos, xy_d, rows_two]).start())
+
+    def ag_c1(p):
+        v = weight_piece(p, core)
+        for k in range(4):
+            from_a(p, k, v).wait_recv()
+        ag_one(p, v, sides(p)[0][1]).start()
+
+    def ag_c4(p):
+        if p:
+            v = weight_piece(p, core)
+            ag_z_from(p, 2, v.at[z_of(2), xy_d, rows_two], 13).wait_recv()
+            pass_to_end(
+                lambda far, k: ag_pass(p, far, k, v.at[far, xy_d, rows_two], 13).start()
+            )
 
     def ag_d(p):
         v = weight_piece(p, core)
-        up, down = pl.ds(0, 2), pl.ds(2, 2)
-        ag_copy(p, 5, v.at[down, xy_d], v.at[down, xy_d], x_dev).wait_recv()
-        ag_copy(p, 6, v.at[up, xy_d], v.at[up, xy_d], y_dev).wait_recv()
-        ag_copy(p, 7, v, v, sib).start()
+        for k in (1, 2, 3) if p else (0, 1, 2, 3):
+            from_b(p, k, v).wait_recv()
+        ag_one(p, v, xy_d).wait_recv()
+        if p:
+            for k in (1, 3):
+                ag_z_from(p, k, v.at[z_of(4 - k), xy_d, rows_two], 13).wait_recv()
+        ag_copy(p, 16, v, v, sib).start()
 
     def ag_e(p):
         v = weight_piece(p, other)
-        ag_copy(p, 7, v, v, sib).wait_recv()
+        ag_copy(p, 16, v, v, sib).wait_recv()
 
     def ag_f(p):
         v = weight_piece(p, core)
-        up = pl.ds(0, 2)
-        for k in (1, 2, 3):
-            ag_copy(p, k - 1, v.at[zpos, xy], v.at[zpos, xy], z_dev(k)).wait_send()
-        ag_copy(p, 3, v.at[:, xy], v.at[:, xy], x_dev).wait_send()
-        ag_copy(p, 4, v.at[:, xy], v.at[:, xy], y_dev).wait_send()
-        ag_copy(p, 5, v.at[up, xy_y], v.at[up, xy_y], x_dev).wait_send()
-        ag_copy(p, 6, v.at[up, xy_x], v.at[up, xy_x], y_dev).wait_send()
-        ag_copy(p, 7, v, v, sib).wait_send()
+        along_z(lambda k: ag_z(p, k, v.at[zpos, xy]).wait_send())
+        pass_to_end(lambda far, k: ag_pass(p, far, k, v.at[far, xy]).wait_send())
+        for k in range(4):
+            ag_x(p, k, v).wait_send()
+            ag_y(p, k, v).wait_send()
+        ag_one(p, v, sides(p)[0][1]).wait_send()
+        if p:
+            ag_two(p, v, sides(p)[1][1]).wait_send()
+            along_z(lambda k: ag_z2(p, k, v.at[zpos, xy_d, rows_two]).wait_send())
+            pass_to_end(
+                lambda far, k: ag_pass(p, far, k, v.at[far, xy_d, rows_two], 13).wait_send()
+            )
+        ag_copy(p, 16, v, v, sib).wait_send()
 
     ahead = 3
 
     def ag_step(s):
-        if s + ahead <= PIECES:
-            ag_a(s + ahead)
-        if s <= PIECES:
-            ag_b(s)
-        if 1 <= s <= PIECES + 1:
-            ag_c(s - 1)
-        if 2 <= s <= PIECES + 2:
-            ag_d(s - 2)
+        for lag, stage in AG_STAGES:
+            if 0 <= s - lag <= PIECES and not (lag < 0 and stage is ag_a and s - lag < ahead):
+                stage(s - lag)
+
+    AG_STAGES = (
+        (-ahead, ag_a),
+        (0, ag_b),
+        (-1, ag_b2),
+        (-1, ag_c2),
+        (0, ag_c3),
+        (1, ag_c1),
+        (1, ag_c4),
+        (2, ag_d),
+    )
 
     order = [9, 10, 11, 12, 5, 6, 7, 8, 4, 1, 2, 3, 0]
 
     def rs_bufs(n):
         if n == PIECES:
             return r.s0, r.s1, r.s2, r.s3
-        q = n % RING
-        return r.l0.at[q], r.l1.at[q], r.l2.at[q], r.l3.at[q]
+        ring = [getattr(r, name).at[n % RINGS[name]] for name in ("l0", "l1", "l2", "l3")]
+        if n >= SHORT:
+            ring[1], ring[3] = r.l1s, r.l3s
+        return tuple(ring)
 
     def rs_copy(n, i, src, dst, dev):
         return remote(src, dst, r.rss.at[n, i], r.rsr.at[n, i], dev)
 
     def credit_wait(n, i):
-        if RING <= n < PIECES:
-            pl.semaphore_wait(r.credit.at[i], 1)
+        if RINGS[CREDIT_RINGS[i]] <= n < (PIECES if i in (0, 3, 4) else SHORT):
+            pl.semaphore_wait(r.credit.at[2 * i + n % 2], 1)
 
     def credit_give(n, i, dev):
-        if n < PIECES - RING:
-            pl.semaphore_signal(r.credit.at[i], inc=1, device_id=(dev,), device_id_type=MESH_ID)
-
-    def add_into(ref, at, landed):
-        ref[at] = (ref[at].astype(F32) + landed.astype(F32)).astype(ref.dtype)
+        if n < (PIECES if i in (0, 3, 4) else SHORT) - RINGS[CREDIT_RINGS[i]]:
+            at = r.credit.at[2 * i + n % 2]
+            pl.semaphore_signal(at, inc=1, device_id=(dev,), device_id_type=MESH_ID)
+
+    def add_to(g, at, landed):
+        g[at] = (g[at].astype(F32) + landed.astype(F32)).astype(g.dtype)
+
+    def z_send(n, first, block, land, k):
+        return rs_copy(n, first + k - 1, block(z_of(k)), land.at[k - 1], z_dev(k))
+
+    def z_far(n, first, block, land, k):
+        return rs_copy(n, first + 3, block(3 if k == 1 else 0), land.at[3], z_dev(k))
+
+    def sum_z_start(n, first, credit, block, land):
+        def near(k):
+            credit_wait(n, credit + k - 1)
+            z_send(n, first, block, land, k).start()
+
+        def far(k):
+            near(2)
+            credit_wait(n, credit + 3)
+            z_far(n, first, block, land, k).start()
+
+        pl.when(jnp.logical_not(at_end))(lambda: near(1))
+        pl.when(jnp.logical_not(at_start))(lambda: near(3))
+        pl.when(at_start)(lambda: far(1))
+        pl.when(at_end)(lambda: far(3))
+
+    def sum_z_pass(n, first, credit, block, land):
+        def go():
+            z_far(n, first, block, land, 1).wait_recv()
+            add_to(block(z_of(2)), Ellipsis, land[3])
+            pl.when(zpos == 1)(lambda: credit_give(n, credit + 3, z_dev(3)))
+            pl.when(zpos == 2)(lambda: credit_give(n, credit + 3, z_dev(1)))
+            credit_wait(n, credit + 1)
+            z_send(n, first, block, land, 2).start()
+
+        pl.when(inside)(go)
+
+    def sum_z_end(n, first, credit, block, land):
+        z_send(n, first, block, land, 2).wait_recv()
+        pl.when(jnp.logical_not(at_start))(lambda: z_send(n, first, block, land, 1).wait_recv())
+        pl.when(jnp.logical_not(at_end))(lambda: z_send(n, first, block, land, 3).wait_recv())
+        total = land[0].astype(F32) + land[1].astype(F32) + land[2].astype(F32)
+
+        def give():
+            credit_give(n, credit + 1, z_dev(2))
+            pl.when(jnp.logical_not(at_start))(lambda: credit_give(n, credit, z_dev(3)))
+            pl.when(jnp.logical_not(at_end))(lambda: credit_give(n, credit + 2, z_dev(1)))
+
+        return total, give
+
+    def sum_z_sent(n, first, block, land):
+        z_send(n, first, block, land, 2).wait_send()
+        pl.when(jnp.logical_not(at_end))(lambda: z_send(n, first, block, land, 1).wait_send())
+        pl.when(jnp.logical_not(at_start))(lambda: z_send(n, first, block, land, 3).wait_send())
+        pl.when(at_start)(lambda: z_far(n, first, block, land, 1).wait_send())
+        pl.when(at_end)(lambda: z_far(n, first, block, land, 3).wait_send())
+
+    def diagonal(n):
+        g = grad_piece(order[n], core)
+        return lambda z: g.at[z, xy_d, rows_two], r.lz.at[n % RINGS["lz"]]
+
+    def own_line(n):
+        g = grad_piece(order[n], core)
+        return lambda z: g.at[z, xy], rs_bufs(n)[3]
+
+    def rs_main(n):
+        p = order[n]
+        g, land = grad_piece(p, core), rs_bufs(n)[2]
+        (a_dev, a), (b_dev, b) = sides(n)
+        one = rs_rows_one(n)
+        early, late_one, late_two = [], [], []
+        if n < SHORT:
+            early.append((7, g.at[:, a, rows_two], land.at[0, :, rows_two], a_dev))
+        late_one.append((8, g.at[:, a, one], land.at[0, :, one], a_dev))
+        early.append((9, g.at[:, b, one], land.at[1, :, one], b_dev))
+        if n < SHORT:
+            for k in (1, 2, 3):
+                z = z_of(k)
+                early.append((9 + k, g.at[z, b, rows_two], land.at[1, z, rows_two], b_dev))
+            late_two.append((13, g.at[zpos, b, rows_two], land.at[1, zpos, rows_two], b_dev))
+        return [[rs_copy(n, *entry) for entry in group] for group in (early, late_one, late_two)]
+
+    def rs_one(n):
+        p = order[n]
+        return rs_copy(
+            n, 1, grad_piece(p, core).at[:, xy_d, rs_rows_one(n)], rs_bufs(n)[1], sides(n)[1][0]
+        )
+
+    def rs_two(n):
+        p = order[n]
+        return rs_copy(
+            n,
+            6,
+            grad_piece(p, core).at[zpos, xy_d, rows_two],
+            r.lt.at[n % RINGS["lt"]],
+            sides(n)[0][0],
+        )
+
+    def rs_swap(n):
+        p = order[n]
+        half = pl.ds(pl.multiple_of(other * 24, 8), 24)
+        return rs_copy(n, 18, r.fs.at[p - 1, half], r.fr.at[p - 1], sib)
 
     def rs_0(n):
+        credit_wait(n, 0)
+        rs_copy(n, 0, grad_piece(order[n], other), rs_bufs(n)[0], sib).start()
+
+    def rs_1(n):
         p = order[n]
         l0 = rs_bufs(n)[0]
-        credit_wait(n, 0)
-        rs_copy(n, 0, grad_piece(p, other), l0, sib).start()
-
-    def rs_1(n):
-        p = order[n]
-        l0, l1, l2, l3 = rs_bufs(n)
         g = grad_piece(p, core)
         rs_copy(n, 0, grad_piece(p, other), l0, sib).wait_recv()
 
@@ -599,53 +808,78 @@
         lax.fori_loop(0, 4, body, 0)
         credit_give(n, 0, sib)
         credit_wait(n, 1)
-        rs_copy(n, 1, g.at[pl.ds(2, 2), xy_d], l1.at[0], x_dev).start()
-        credit_wait(n, 2)
-        rs_copy(n, 2, g.at[pl.ds(0, 2), xy_d], l1.at[1], y_dev).start()
+        rs_one(n).start()
+        if n < SHORT:
+            sum_z_start(n, 2, 5, *diagonal(n))
+        credit_wait(n, 3)
+        credit_wait(n, 4)
+        for copy in rs_main(n)[0]:
+            copy.start()
 
     def rs_2(n):
         p = order[n]
-        l0, l1, l2, l3 = rs_bufs(n)
-        g = grad_piece(p, core)
-        rs_copy(n, 1, g.at[pl.ds(2, 2), xy_d], l1.at[0], x_dev).wait_recv()
-        for i in range(2):
-            g[2 + i, xy_y] = (g[2 + i, xy_y].astype(F32) + l1[0, i].astype(F32)).astype(g.dtype)
-        credit_give(n, 1, x_dev)
-        rs_copy(n, 2, g.at[pl.ds(0, 2), xy_d], l1.at[1], y_dev).wait_recv()
-        for i in range(2):
-            g[i, xy_x] = (g[i, xy_x].astype(F32) + l1[1, i].astype(F32)).astype(g.dtype)
-        credit_give(n, 2, y_dev)
-        credit_wait(n, 3)
-        rs_copy(n, 3, g.at[:, xy_x], l2.at[0], x_dev).start()
-        credit_wait(n, 4)
-        rs_copy(n, 4, g.at[:, xy_y], l2.at[1], y_dev).start()
+        g, l1 = grad_piece(p, core), rs_bufs(n)[1]
+        (a_dev, a), (b_dev, b) = sides(n)
+        rs_one(n).wait_recv()
+        for z in range(4):
+            add_to(g, (z, a, rs_rows_one(n)), l1[z])
+        credit_give(n, 1, b_dev)
+        for copy in rs_main(n)[1]:
+            copy.start()
+        if n < SHORT:
+            sum_z_pass(n, 2, 5, *diagonal(n))
 
     def rs_3(n):
         p = order[n]
-        l0, l1, l2, l3 = rs_bufs(n)
-        g = grad_piece(p, core)
-        rs_copy(n, 3, g.at[:, xy_x], l2.at[0], x_dev).wait_recv()
-        rs_copy(n, 4, g.at[:, xy_y], l2.at[1], y_dev).wait_recv()
-        for i in range(4):
-            g[i, xy] = (
-                g[i, xy].astype(F32) + l2[0, i].astype(F32) + l2[1, i].astype(F32)
-            ).astype(g.dtype)
-        credit_give(n, 3, x_dev)
-        credit_give(n, 4, y_dev)
-        for k in (1, 2, 3):
-            credit_wait(n, 4 + k)
-            rs_copy(n, 4 + k, g.at[z_of(k), xy], l3.at[k - 1], z_dev(k)).start()
+        if p:
+            g = grad_piece(p, core)
+            total, give = sum_z_end(n, 2, 5, *diagonal(n))
+            add_to(g, (zpos, xy_d, rows_two), total)
+            give()
+            credit_wait(n, 2)
+            rs_two(n).start()
 
     def rs_4(n):
         p = order[n]
-        l0, l1, l2, l3 = rs_bufs(n)
-        g = grad_piece(p, core)
-        total = g[zpos, xy].astype(F32)
-        for k in (1, 2, 3):
-            rs_copy(n, 4 + k, g.at[z_of(k), xy], l3.at[k - 1], z_dev(k)).wait_recv()
-            total = total + l3[k - 1].astype(F32)
-        for k in (1, 2, 3):
-            credit_give(n, 4 + k, z_dev(4 - k))
+        if p:
+            g = grad_piece(p, core)
+            (a_dev, a), (b_dev, b) = sides(n)
+            rs_two(n).wait_recv()
+            add_to(g, (zpos, b, rows_two), r.lt[n % RINGS["lt"]])
+            credit_give(n, 2, a_dev)
+            for copy in rs_main(n)[2]:
+                copy.start()
+
+    def rs_5(n):
+        p = order[n]
+        g, l2 = grad_piece(p, core), rs_bufs(n)[2]
+        (a_dev, a), (b_dev, b) = sides(n)
+        for group in rs_main(n):
+            for copy in group:
+                copy.wait_recv()
+        for z in range(4):
+            add_to(g, (z, xy), l2[0, z].astype(F32) + l2[1, z].astype(F32))
+        credit_give(n, 3, a_dev)
+        credit_give(n, 4, b_dev)
+        if n < SHORT:
+            sum_z_start(n, 14, 9, *own_line(n))
+        else:
+            for k in (1, 2, 3):
+                z_send(n, 14, *own_line(n), k).start()
+
+    def rs_6(n):
+        sum_z_pass(n, 14, 9, *own_line(n))
+
+    def rs_7(n):
+        p = order[n]
+        if n < SHORT:
+            total, give = sum_z_end(n, 14, 9, *own_line(n))
+        else:
+            land = rs_bufs(n)[3]
+            for k in (1, 2, 3):
+                z_send(n, 14, *own_line(n), k).wait_recv()
+            total = land[0].astype(F32) + land[1].astype(F32) + land[2].astype(F32)
+        total = total + grad_piece(p, core)[zpos, xy].astype(F32)
         if p == 0:
             r.osm[...] = total
         elif p >= 9:
@@ -653,20 +887,20 @@
             r.o2[ROWS * i : ROWS * (i + 1), COLS * j : COLS * (j + 1)] = total
         else:
             r.fs[p - 1] = total
-            half = pl.ds(pl.multiple_of(other * 24, 8), 24)
-            rs_copy(n, 8, r.fs.at[p - 1, half], r.fr.at[p - 1], sib).start()
-
-    def rs_5(n):
+            rs_swap(n).start()
+        if n < SHORT:
+            give()
+
+    def rs_8(n):
         p = order[n]
         if p == 0 or p >= 9:
             return
-        half = pl.ds(pl.multiple_of(other * 24, 8), 24)
         mine = pl.ds(pl.multiple_of(core * 24, 8), 24)
-        rs_copy(n, 8, r.fs.at[p - 1, half], r.fr.at[p - 1], sib).wait_recv()
-        out, first = (r.oq, p - 1) if p <= 3 else ((r.op, 0) if p == 4 else (r.o1, p - 5))
+        rs_swap(n).wait_recv()
+        out, first = (r.oq, 0) if p <= 3 else ((r.op, 0) if p == 4 else (r.o1, p - 5))
         for g in range(3):
             lanes = slice(LANES * g, LANES * (g + 1))
-            base = 768 * first + 256 * g
+            base = 768 * g + 256 * (p - 1) if p <= 3 else 768 * first + 256 * g
             out[:, pl.ds(pl.multiple_of(base + LANES * core, LANES), LANES)] = r.fs[
                 p - 1, mine, lanes
             ]
@@ -674,29 +908,33 @@
                 p - 1, :, lanes
             ]
 
-    def rs_6(n):
+    def rs_9(n):
         p = order[n]
-        l0, l1, l2, l3 = rs_bufs(n)
-        g = grad_piece(p, core)
-        rs_copy(n, 0, grad_piece(p, other), l0, sib).wait_send()
-        rs_copy(n, 1, g.at[pl.ds(2, 2), xy_d], l1.at[0], x_dev).wait_send()
-        rs_copy(n, 2, g.at[pl.ds(0, 2), xy_d], l1.at[1], y_dev).wait_send()
-        rs_copy(n, 3, g.at[:, xy_x], l2.at[0], x_dev).wait_send()
-        rs_copy(n, 4, g.at[:, xy_y], l2.at[1], y_dev).wait_send()
-        for k in (1, 2, 3):
-            rs_copy(n, 4 + k, g.at[z_of(k), xy], l3.at[k - 1], z_dev(k)).wait_send()
+        rs_copy(n, 0, grad_piece(p, other), rs_bufs(n)[0], sib).wait_send()
+        rs_one(n).wait_send()
+        for group in rs_main(n):
+            for copy in group:
+                copy.wait_send()
+        if n < SHORT:
+            sum_z_sent(n, 2, *diagonal(n))
+            rs_two(n).wait_send()
+            sum_z_sent(n, 14, *own_line(n))
+        else:
+            for k in (1, 2, 3):
+                z_send(n, 14, *own_line(n), k).wait_send()
         if 1 <= p <= 8:
-            half = pl.ds(pl.multiple_of(other * 24, 8), 24)
-            rs_copy(n, 8, r.fs.at[p - 1, half], r.fr.at[p - 1], sib).wait_send()
-
-    rs_stages = (rs_0, rs_1, rs_2, rs_3, rs_4, rs_5, rs_6)
-
-    base = [0, 1, 2, 3, 6, 7, 8, 9, 10, 14, 15, 16, 18]
+            rs_swap(n).wait_send()
+
+    rs_long = (rs_0, rs_1, rs_2, rs_3, rs_4, rs_5, rs_6, rs_7, rs_8, rs_9)
+    rs_short = (rs_0, rs_1, rs_2, rs_5, rs_7, rs_8, rs_9)
+
+    base = [0, 1, 2, 3, 4, 5, 6, 7, 8, 9, 10, 12, 14]
 
     def rs_step(s):
-        for i, stage in enumerate(rs_stages):
-            if s - i in base:
-                stage(base.index(s - i))
+        for n in range(PIECES + 1):
+            stages = rs_long if n < SHORT else rs_short
+            if 0 <= s - base[n] < len(stages):
+                stages[s - base[n]](n)
 
     def rows_of(f):
         return pl.ds(pl.multiple_of(f * WIN, WIN), WIN)
@@ -756,14 +994,17 @@
         r.dm[rw, :] = (r.dm[rw, :].astype(F32) * r.st[rw, 1:2]).astype(BF16)
 
     def spread_small():
-        table = r.sv[...].reshape(32, 16, LANES).astype(F32)
+        table = r.sv[...].reshape(32, 8, LANES)
         rows = [table[:, i, :].astype(BF16) for i in range(3)]
         at = 0
         for name, row, lane0, width in SMALL_ROWS:
             pick, owner = spread_tables(lane0, width)
             full = jnp.sum(jnp.where(owner, dot_nn(rows[row], pick), 0.0), axis=0, keepdims=True)
             if name == "qkv_bias":
-                r.bqkv[...] = full
+                for t in range(3):
+                    for g in range(3):
+                        at_piece, at_whole = 768 * t + 256 * g, 768 * g + 256 * t
+                        r.bqkv[:, at_piece : at_piece + 256] = full[:, at_whole : at_whole + 256]
             elif name == "fc1_bias":
                 r.bfc1[...] = full
             else:
@@ -777,7 +1018,8 @@
         for name, row, lane0, width in SMALL_ROWS:
             pick, owner = spread_tables(lane0, width)
             if name == "qkv_bias":
-                full = r.gbqkv[...]
+                chunks = [768 * t + 256 * g for g in range(3) for t in range(3)]
+                full = jnp.concatenate([r.gbqkv[:, c : c + 256] for c in chunks], axis=1)
             elif name == "fc1_bias":
                 full = r.gbfc1[...]
             else:
@@ -803,42 +1045,52 @@
 
     def qkv(t):
         w = jnp.concatenate(natural(wa_m, (t,), pl.ds(0, 768)), axis=1)
-        cols = slice(768 * t, 768 * (t + 1))
+        cols = tile(t)
         bias = r.bqkv[:, cols]
         for i in range(4):
             s = slice(WIN * i, WIN * (i + 1))
             r.packed[s, cols] = (dot_nn(r.normed[s, :], w) + bias).astype(BF16)
 
+    def part(t, i, pair):
+        return pl.ds(pl.multiple_of(768 * t + 256 * i + LANES * pair, LANES), LANES)
+
+    def head_cols(t, pair):
+        return pl.ds(pl.multiple_of(256 * t + LANES * pair, LANES), LANES)
+
     low_lanes = lax.broadcasted_iota(jnp.int32, (WIN, LANES), 1) < HEAD_DIM
 
     def two_heads(a):
         z = jnp.zeros_like(a)
         return jnp.concatenate([jnp.where(low_lanes, a, z), jnp.where(low_lanes, z, a)], axis=0)
 
-    def attention(f):
+    def attention(t, f, pair):
         rw = rows_of(f)
-        for hp in range(HEADS // 2):
-            part = lambda i: slice(768 * i + LANES * hp, 768 * i + LANES * (hp + 1))
-            q2 = r.packed[rw, part(0)] * jnp.asarray(0.125, BF16)
-            k2 = r.packed[rw, part(1)]
-            v2 = r.packed[rw, part(2)]
-            scores = dot_nt(two_heads(q2), k2)
-            row_max = jnp.max(scores, axis=1, keepdims=True)
-            e = jnp.exp(scores - row_max)
-            total = jnp.sum(e, axis=1, keepdims=True)
-            inv = 1.0 / total
-            log_total = row_max + jnp.log(total)
-            for h in range(2):
-                col = jnp.broadcast_to(log_total[WIN * h : WIN * (h + 1)], (WIN, 8))
-                r.lse[f * 6 + hp, h : h + 1, :] = jnp.transpose(col)[0:1]
-            e = e.astype(BF16)
-            out = dot_nn(jnp.concatenate([e[:WIN], e[WIN:]], axis=1), two_heads(v2))
-            scale = jnp.where(
-                low_lanes,
-                jnp.broadcast_to(inv[:WIN], (WIN, LANES)),
-                jnp.broadcast_to(inv[WIN:], (WIN, LANES)),
-            )
-            r.att[rw, part(0)] = (out * scale).astype(BF16)
+        q2 = r.packed[rw, part(t, 0, pair)] * jnp.asarray(0.125, BF16)
+        k2 = r.packed[rw, part(t, 1, pair)]
+        v2 = r.packed[rw, part(t, 2, pair)]
+        scores = dot_nt(two_heads(q2), k2)
+        row_max = jnp.max(scores, axis=1, keepdims=True)
+        e = jnp.exp(scores - row_max)
+        total = jnp.sum(e, axis=1, keepdims=True)
+        inv = 1.0 / total
+        log_total = row_max + jnp.log(total)
+        for h in range(2):
+            col = jnp.broadcast_to(log_total[WIN * h : WIN * (h + 1)], (WIN, 8))
+            r.lse[f * 6 + 2 * t + pair, h : h + 1, :] = jnp.transpose(col)[0:1]
+        e = e.astype(BF16)
+        out = dot_nn(jnp.concatenate([e[:WIN], e[WIN:]], axis=1), two_heads(v2))
+        scale = jnp.where(
+            low_lanes,
+            jnp.broadcast_to(inv[:WIN], (WIN, LANES)),
+            jnp.broadcast_to(inv[WIN:], (WIN, LANES)),
+        )
+        r.att[rw, head_cols(t, pair)] = (out * scale).astype(BF16)
+
+    def heads_forward(t):
+        qkv(t)
+        for f in range(4):
+            for pair in range(2):
+                attention(t, f, pair)
 
     def project(f):
         rw = rows_of(f)
@@ -942,28 +1194,32 @@
         w = jnp.concatenate(natural(wa_m, (3,), pl.ds(0, 768)), axis=1)
         r.n2[rw, :] = dot_nt(r.dm[rw, :], w).astype(BF16)
 
-    def attention_backward(f):
+    def attention_backward(t, f, pair):
         rw = rows_of(f)
-        for hp in range(HEADS // 2):
-            part = lambda i: slice(768 * i + LANES * hp, 768 * i + LANES * (hp + 1))
-            q2 = r.packed[rw, part(0)] * jnp.asarray(0.125, BF16)
-            k2 = r.packed[rw, part(1)]
-            v2 = r.packed[rw, part(2)]
-            qs, ds, ks = two_heads(q2), two_heads(r.n2[rw, part(0)]), two_heads(k2)
-            log_total = jnp.concatenate(
-                [r.lse[f * 6 + hp, 0:1, :], r.lse[f * 6 + hp, 1:2, :]], axis=1
-            )
-            probs = jnp.exp(dot_nt(k2, qs) - log_total)
-            prod = probs * dot_nt(v2, ds)
-            row_dot = jnp.sum(prod, axis=0, keepdims=True)
-            d_scores = (prod - probs * row_dot).astype(BF16)
-            r.packed[rw, part(2)] = dot_nn(probs.astype(BF16), ds).astype(BF16)
-            r.packed[rw, part(1)] = dot_nn(d_scores, qs).astype(BF16)
-            stacked = jnp.concatenate([d_scores[:, :WIN], d_scores[:, WIN:]], axis=0)
-            r.packed[rw, part(0)] = (dot_tn(stacked, ks) * 0.125).astype(BF16)
+        q2 = r.packed[rw, part(t, 0, pair)] * jnp.asarray(0.125, BF16)
+        k2 = r.packed[rw, part(t, 1, pair)]
+        v2 = r.packed[rw, part(t, 2, pair)]
+        qs, ds, ks = two_heads(q2), two_heads(r.n2[rw, head_cols(t, pair)]), two_heads(k2)
+        at = f * 6 + 2 * t + pair
+        log_total = jnp.concatenate([r.lse[at, 0:1, :], r.lse[at, 1:2, :]], axis=1)
+        probs = jnp.exp(dot_nt(k2, qs) - log_total)
+        prod = probs * dot_nt(v2, ds)
+        row_dot = jnp.sum(prod, axis=0, keepdims=True)
+        d_scores = (prod - probs * row_dot).astype(BF16)
+        r.packed[rw, part(t, 2, pair)] = dot_nn(probs.astype(BF16), ds).astype(BF16)
+        r.packed[rw, part(t, 1, pair)] = dot_nn(d_scores, qs).astype(BF16)
+        stacked = jnp.concatenate([d_scores[:, :WIN], d_scores[:, WIN:]], axis=0)
+        r.packed[rw, part(t, 0, pair)] = (dot_tn(stacked, ks) * 0.125).astype(BF16)
+
+    def heads_backward(t):
+        def body(f):
+            for pair in range(2):
+                attention_backward(t, f, pair)
+
+        return body
 
     def grad_qkv(t):
-        cols = slice(768 * t, 768 * (t + 1))
+        cols = tile(t)
         d = r.packed[:, cols]
         put_a(t, slice(None), dot_nn(r.tr[...], d).astype(BF16))
         r.gbqkv[:, cols] = jnp.sum(d.astype(F32), axis=0, keepdims=True)
@@ -1004,16 +1260,21 @@
     for copy in loads:
         copy.start()
 
+    for land in (r.lz, r.l3):
+        for slot in range(land.shape[0]):
+            land[slot, 0] = jnp.zeros_like(land[slot, 0])
+            land[slot, 2] = jnp.zeros_like(land[slot, 2])
+
     barrier = pltpu.get_barrier_semaphore()
     peers = [sib, x_dev, y_dev, z_dev(1), z_dev(2), z_dev(3)]
     for dev in peers:
         pl.semaphore_signal(barrier, inc=1, device_id=(dev,), device_id_type=MESH_ID)
 
     def shard_half(t, half):
-        ref, first = (r.sq, t) if t < 3 else ((r.sp, 0) if t == 3 else (r.s1w, t - 4))
+        ref, first = (r.sq, 0) if t < 3 else ((r.sp, 0) if t == 3 else (r.s1w, t - 4))
         parts = []
         for g in range(3):
-            base = 768 * first + 256 * g
+            base = 768 * g + 256 * t if t < 3 else 768 * first + 256 * g
             a = ref[:, base : base + LANES].astype(F32)
             b = ref[:, base + LANES : base + 2 * LANES].astype(F32)
             parts.append(jnp.where(half == 0, a, b))
@@ -1021,16 +1282,17 @@
 
     for t in range(8):
         away = jnp.concatenate([shard_half(t, other), jnp.zeros((8, COLS), F32)], axis=0)
-        r.tx[t] = away.astype(BF16)
+        r.l0[0, t // 4, t % 4, 0:32] = away.astype(BF16)
     pl.semaphore_wait(barrier, len(peers))
-    swap = remote(r.tx, r.rx, r.prep.at[0], r.prep.at[1], sib)
+    away, came = [r.l0.at[i, pl.ds(0, 2), :, pl.ds(0, 32)] for i in range(2)]
+    swap = remote(away, came, r.prep.at[0], r.prep.at[1], sib)
     swap.start()
     loads[4].wait()
     ag_a(0)
     swap.wait()
     for t in range(8):
         here = shard_half(t, core)
-        there = r.rx[t].astype(F32)[:24]
+        there = r.l0[1, t // 4, t % 4, 0:32].astype(F32)[:24]
         block = jnp.concatenate(
             [jnp.where(core == 0, here, there), jnp.where(core == 0, there, here)], axis=0
         ).astype(BF16)
@@ -1038,10 +1300,32 @@
             wa_v[core, t, zpos, xy] = block
         else:
             w1_v[core, t - 4, zpos, xy] = block
-    for p in range(1, ahead):
-        ag_a(p)
+        if t + 1 < ahead:
+            ag_a(t + 1)
+    ag_step(-1)
     loads[2].wait()
     loads[3].wait()
+    def ag(*numbers):
+        def go():
+            for s in numbers:
+                ag_step(s)
+
+        return go
+
+    def rs(*numbers):
+        def go():
+            for s in numbers:
+                rs_step(s)
+
+        return go
+
+    def arrive(p, *numbers):
+        def go():
+            ag(*numbers)()
+            ag_e(p)
+
+        return go
+
     ag_step(0)
     masks()
     ag_step(1)
@@ -1049,75 +1333,84 @@
     loop(4, mask_grad)
     ag_step(2)
     ag_e(0)
+    ag_step(3)
     loads[1].wait()
     spread_small()
-    ag_step(3)
     loop(4, ln1)
     ag_e(1)
-    qkv(0)
-    ag_step(4)
-    ag_e(2)
-    qkv(1)
-    ag_step(5)
-    ag_e(3)
-    qkv(2)
-    ag_step(6)
-    loop(4, attention, steps(ag_step, None, 7, 8, 9))
-    ag_e(4)
-    loop(4, project)
+    loop(3, heads_forward, [arrive(2, 4), arrive(3, 5), ag(6)])
+    arrive(4)()
+    loop(4, project, [None, ag(7), None, None])
     keep_middle = pltpu.make_async_copy(r.mid, r.ig, r.ld.at[5])
     keep_middle.start()
-
-    def arrive(p, s=None):
-        def go():
-            if s is not None:
-                ag_step(s)
-            ag_e(p)
-
-        return go
-
     arrive(5)()
-    loop(4, fc1, [arrive(6, 10), arrive(7, 11), arrive(8), functools.partial(ag_step, 12)])
+    loop(4, fc1, [arrive(6, 8), arrive(7, 9), arrive(8, 10), ag(11)])
     loop(4, turn(1))
-    loop(4, grad_fc2, steps(ag_step, None, 13, None, 14))
+    loop(4, grad_fc2, [ag(12), None, ag(13), ag(14)])
     rs_step(0)
     for p in range(PIECES + 1):
         if p >= 9:
             ag_e(p)
         ag_f(p)
     rs_step(1)
-    loop(4, grad_pre, steps(rs_step, None, 2, None, 3))
-    loop(3, grad_norm_two, steps(rs_step, 4, None, 5))
-    loop(4, grad_fc1, steps(rs_step, 6, None, None, 7))
+    loop(4, grad_pre, [None, None, rs(2), None])
+    loop(3, grad_norm_two, [rs(3), None, None])
+    loop(4, grad_fc1, [rs(4), None, None, rs(5)])
     keep_middle.wait()
     loop(4, grad_middle)
-    rs_step(8)
     loop(3, grad_proj)
+    rs_step(6)
     loop(4, grad_att)
-    rs_step(9)
-    loop(4, attention_backward, steps(rs_step, 10, 11, 12, 13))
     loop(4, turn(0))
-    for t in range(3):
-        grad_qkv(t)
-        rs_step(14 + t)
-    loop(3, grad_norm_one, steps(rs_step, None, 17, None))
+    loop(4, heads_backward(0), [rs(7), None, None, rs(8)])
+    grad_qkv(0)
+    loop(4, heads_backward(1), [None, rs(9), None, None])
+    grad_qkv(1)
+    rs_step(10)
+    loop(4, heads_backward(2), [None, None, rs(11), None])
+    grad_qkv(2)
+    rs_step(12)
+    loop(3, grad_norm_one, [None, None, rs(13)])
     loop(4, grad_mixed)
-    collect_small()
     load_middle = pltpu.make_async_copy(r.ig, r.mid, r.ld.at[6])
     load_middle.start()
-    rs_step(18)
+    collect_small()
+    rs_step(14)
     load_middle.wait()
     write_grad = pltpu.make_async_copy(r.dn, r.ig, r.ld.at[7])
     write_grad.start()
-    loop(3, fc2, steps(rs_step, 19, 20, None))
+    loop(3, fc2, [rs(15), rs(16), rs(17)])
     write_out = pltpu.make_async_copy(r.n2, r.bo, r.ld.at[0])
     write_out.start()
-    rs_step(21)
-    rs_step(22)
-    rs_step(23)
-    rs_step(24)
+    for s in range(18, 21):
+        rs_step(s)
     write_grad.wait()
     write_out.wait()
+
+
+HAND_PARTS = 4
+
+
+def hand_over(*refs):
+    arrays, small, outs = refs[:6], refs[6], refs[7:13]
+    vectors, held, (in_sems, out_sems) = refs[13:-8], refs[-8:-2], refs[-2:]
+    loads, stores = [], []
+    for src, buf, dst in zip(arrays, held, outs):
+        parts = HAND_PARTS if src.shape[0] == 1024 else 1
+        rows = src.shape[0] // parts
+        for i in range(parts):
+            at, n = pl.ds(rows * i, rows), len(loads)
+            loads.append(pltpu.make_async_copy(src.at[at], buf.at[at], in_sems.at[n]))
+            stores.append(pltpu.make_async_copy(buf.at[at], dst.at[at], out_sems.at[n]))
+    for copy in loads:
+        copy.start()
+    for ref, (_, row, lane0, width) in zip(vectors, SMALL_ROWS):
+        ref[...] = small[row : row + 1, lane0 : lane0 + width]
+    for load, store in zip(loads, stores):
+        load.wait()
+        store.start()
+    for copy in stores:
+        copy.wait()
 
 
 def fused_device(
@@ -1139,11 +1432,22 @@
     mask_embed,
     out_grad,
 ):
-    pad = jnp.zeros((8,), BF16)
-    small = jnp.concatenate(
-        [ln1_gain, ln1_bias, proj_bias, ln2_gain, ln2_bias, pad, fc2_bias, mask_embed, qkv_bias]
-        + [pad, fc1_bias, jnp.zeros((32 + 13 * LANES,), BF16)]
-    ).reshape(16, LANES)
+    held = dict(
+        ln1_gain=ln1_gain,
+        ln1_bias=ln1_bias,
+        proj_bias=proj_bias,
+        ln2_gain=ln2_gain,
+        ln2_bias=ln2_bias,
+        fc2_bias=fc2_bias,
+        mask_embed=mask_embed,
+        qkv_bias=qkv_bias,
+        fc1_bias=fc1_bias,
+    )
+    small = jnp.zeros((8 * LANES,), F32)
+    for name, row, lane0, width in SMALL_ROWS:
+        first = row * LANES + lane0
+        small = small + jnp.pad(held[name].astype(F32), (first, 8 * LANES - first - width))
+    small = small.reshape(8, LANES)
     any_spec = pl.BlockSpec(memory_space=pl.ANY)
     vmem = pl.BlockSpec(memory_space=pltpu.VMEM)
     smem = pl.BlockSpec(memory_space=pltpu.SMEM)
@@ -1176,8 +1480,18 @@
         fc1_weight,
         fc2_weight,
     )
-    block_out, input_grad, gq, gpj, g1, g2, gsmall = outs
-    v = {name: gsmall[row, lane : lane + width] for name, row, lane, width in SMALL_ROWS}
+    held = pl.pallas_call(
+        hand_over,
+        out_shape=tuple(shape(o.shape, o.dtype) for o in outs[:6])
+        + tuple(shape((1, width), F32) for _, _, _, width in SMALL_ROWS),
+        in_specs=[any_spec] * 6 + [vmem],
+        out_specs=(any_spec,) * 6 + (vmem,) * len(SMALL_ROWS),
+        scratch_shapes=[pltpu.VMEM(o.shape, o.dtype) for o in outs[:6]]
+        + [pltpu.SemaphoreType.DMA((6 * HAND_PARTS,)), pltpu.SemaphoreType.DMA((6 * HAND_PARTS,))],
+        compiler_params=pltpu.CompilerParams(vmem_limit_bytes=63 * 2**20),
+    )(*outs)
+    block_out, input_grad, gq, gpj, g1, g2 = held[:6]
+    v = {entry[0]: vec.reshape(entry[3]) for entry, vec in zip(SMALL_ROWS, held[6:])}
     return (
         block_out,
         input_grad,

time: 202 us -> 182 us (0.901)
  local copies, waits for them, and re-layouts: 17.9 us -> 0 us
  Pallas kernels: 183 us -> 180 us
    pallas_call x1, Pallas kernels: 183 us -> 173 us  [fused_device(): pl.pallas_call(fused_kernel, out_shape=(shape((1024, 768), BF16), shape((...]
    unnamed x16 -> x0, local copies, waits for them, and re-layouts: 7.23 us -> none
    concatenate x1 -> x0, local copies, waits for them, and re-layouts: 6.69 us -> none  [fused_device(): jnp.concatenate([ln1_gain, ln1_bias, proj_bias, ln2_gain, ln2_bias, pad,...]
    pallas_call x0 -> x1, Pallas kernels: none -> 6.35 us  [fused_device(): pl.pallas_call(hand_over, out_shape=tuple((shape(o.shape, o.dtype) for o...]
    squeeze x3 -> x0, local copies, waits for them, and re-layouts: 3.99 us -> none  [fused_device(): gsmall[row, lane:lane + width]]
where the time goes in v2:
time: 182 us
  Pallas kernels  180 us (99%)
    pallas_call x1, Pallas kernels, fused_device(): pl.pallas_call(fused_kernel, out_shape=(shape((1024, 768), BF16), shape((...  173 us
    pallas_call x1, Pallas kernels, fused_device(): pl.pallas_call(hand_over, out_shape=tuple((shape(o.shape, o.dtype) for o...  6.35 us

profile of v2, /device:TPU:0, one launch (start us, length us, event | category | flops | bytes accessed | tf_op | source)
XLA Modules:
  0.0 182.1 jit_solution(10671784489150129050)
XLA Ops:
  0.6 1.5 add_bitcast_fusion.refs_4_
  2.1 173.5 %shard_map.280 = (bf16[1024,768]{1,0:T(8,128)(2,1)}, f32[1024,768]{1,0:T(8,128)}, f32[24,2304]{1,0:T(8,128)}, f32[24,768]{1,0:T(8,128)}, f32[24,3072]{1,0:T(8,12...) custom-call(bf16[1024,768]{1,0:T(8,128)(2,1)} %refs_0_.1, bf16[1024,768]{1,0:T(8,128)(2,1)} %refs_1_.1, s32[8,128]{1,0:T(8,128)} %bitcast.12, ...), custom_call_target="tpu_custom_call" | custom-call | tf_op jit(solution)/shard_map/pallas_call | solution.py:1455
  175.6 6.4 %shard_map.281 = (bf16[1024,768]{1,0:T(8,128)(2,1)}, f32[1024,768]{1,0:T(8,128)}, f32[24,2304]{1,0:T(8,128)}, f32[24,768]{1,0:T(8,128)}, f32[24,3072]{1,0:T(8,12...) custom-call(bf16[1024,768]{1,0:T(8,128)(2,1)} %get-tuple-element.37., ...), custom_call_target="tpu_custom_call" | custom-call | tf_op jit(solution)/shard_map/pallas_call | solution.py:1483

commit v3 on v2

--- a/solution.py
+++ b/solution.py
@@ -322,6 +322,9 @@
 RINGS = dict(l0=2, l1=4, lz=4, lt=4, l2=4, l3=4)
 CREDIT_RINGS = ["l0", "l1", "lt", "l2", "l2"] + ["lz"] * 4 + ["l3"] * 4
 SHORT = 11
+LONG_AT = (0, 2, 5, 8, 11, 14, 17, 20, 22, 23)
+SHORT_AT = (0, 2, 5, 8, 11, 13, 14)
+STARTS = (0, 1, 3, 5, 8, 10, 13, 16, 19, 22, 25, 30, 36)
 MESH_ID = pl.DeviceIdType.MESH
 
 
@@ -424,11 +427,9 @@
 SEMS = dict(
     ld=pltpu.SemaphoreType.DMA((8,)),
     prep=pltpu.SemaphoreType.DMA((2,)),
-    ags=pltpu.SemaphoreType.DMA((PIECES + 1, 17)),
-    agr=pltpu.SemaphoreType.DMA((PIECES + 1, 17)),
-    rss=pltpu.SemaphoreType.DMA((PIECES + 1, 19)),
-    rsr=pltpu.SemaphoreType.DMA((PIECES + 1, 19)),
-    credit=pltpu.SemaphoreType.REGULAR((32,)),
+    sent=pltpu.SemaphoreType.DMA((PIECES + 1, 14)),
+    came=pltpu.SemaphoreType.DMA((PIECES + 1, 14)),
+    credit=pltpu.SemaphoreType.REGULAR((26,)),
 )
 
 
@@ -506,7 +507,7 @@
         return g2_v.at[(p - 9) % 2, :, :, half, (p - 9) // 2]
 
     def ag_copy(p, i, src, dst, dev):
-        return remote(src, dst, r.ags.at[p, i], r.agr.at[p, i], dev)
+        return remote(src, dst, r.sent.at[p, i], r.came.at[p, i], dev)
 
     def rows_one(p):
         return pl.ds(0, CUT) if p else pl.ds(0, 8)
@@ -536,7 +537,7 @@
         return ag_copy(p, k - 1, at, at, z_dev(k))
 
     def ag_z2(p, k, at):
-        return ag_copy(p, 12 + k, at, at, z_dev(k))
+        return ag_copy(p, 8 + k, at, at, z_dev(k))
 
     def ag_z_from(p, k, at, base=0):
         return ag_copy(p, base + k - 1, at, at, z_dev(k))
@@ -546,33 +547,27 @@
 
     def ag_x(p, k, v):
         at = v.at[z_of(4 - k), xy] if k else v.at[zpos, xy]
-        return ag_copy(p, 3 + k, at, at, x_dev)
+        return ag_copy(p, 4 if k else 3, at, at, x_dev)
 
     def ag_y(p, k, v):
         at = v.at[z_of(4 - k), xy] if k else v.at[zpos, xy]
-        return ag_copy(p, 7 + k, at, at, y_dev)
-
-    def from_x(p, k, v):
-        at = v.at[z_of(4 - k), xy_x] if k else v.at[zpos, xy_x]
-        return ag_copy(p, 3 + k, at, at, x_dev)
-
-    def from_y(p, k, v):
-        at = v.at[z_of(4 - k), xy_y] if k else v.at[zpos, xy_y]
-        return ag_copy(p, 7 + k, at, at, y_dev)
-
-    def from_a(p, k, v):
-        return from_x(p, k, v) if p % 2 == 0 else from_y(p, k, v)
-
-    def from_b(p, k, v):
-        return from_y(p, k, v) if p % 2 == 0 else from_x(p, k, v)
+        return ag_copy(p, 6 if k else 5, at, at, y_dev)
+
+    def own_from(p, side, v):
+        at = v.at[zpos, sides(p)[side][1]]
+        return ag_copy(p, 3 if side == p % 2 else 5, at, at, sides(p)[side][0])
+
+    def three_from(p, side, v):
+        at = v.at[pl.ds(0, 3), sides(p)[side][1]]
+        return ag_copy(p, 4 if side == p % 2 else 6, at, at, sides(p)[side][0])
 
     def ag_one(p, v, col):
         at = v.at[:, col, rows_one(p)]
-        return ag_copy(p, 11, at, at, sides(p)[1][0])
+        return ag_copy(p, 7, at, at, sides(p)[1][0])
 
     def ag_two(p, v, col):
         at = v.at[zpos, col, rows_two]
-        return ag_copy(p, 12, at, at, sides(p)[0][0])
+        return ag_copy(p, 8, at, at, sides(p)[0][0])
 
     def ag_a(p):
         v = weight_piece(p, core)
@@ -597,7 +592,7 @@
     def ag_c2(p):
         if p:
             v = weight_piece(p, core)
-            from_b(p, 0, v).wait_recv()
+            own_from(p, 1, v).wait_recv()
             ag_two(p, v, sides(p)[1][1]).start()
 
     def ag_c3(p):
@@ -608,47 +603,50 @@
 
     def ag_c1(p):
         v = weight_piece(p, core)
-        for k in range(4):
-            from_a(p, k, v).wait_recv()
+        own_from(p, 0, v).wait_recv()
+        three_from(p, 0, v).wait_recv()
         ag_one(p, v, sides(p)[0][1]).start()
 
     def ag_c4(p):
         if p:
             v = weight_piece(p, core)
-            ag_z_from(p, 2, v.at[z_of(2), xy_d, rows_two], 13).wait_recv()
+            ag_z_from(p, 2, v.at[z_of(2), xy_d, rows_two], 9).wait_recv()
             pass_to_end(
-                lambda far, k: ag_pass(p, far, k, v.at[far, xy_d, rows_two], 13).start()
+                lambda far, k: ag_pass(p, far, k, v.at[far, xy_d, rows_two], 9).start()
             )
 
     def ag_d(p):
         v = weight_piece(p, core)
-        for k in (1, 2, 3) if p else (0, 1, 2, 3):
-            from_b(p, k, v).wait_recv()
+        if p == 0:
+            own_from(p, 1, v).wait_recv()
+        three_from(p, 1, v).wait_recv()
         ag_one(p, v, xy_d).wait_recv()
         if p:
             for k in (1, 3):
-                ag_z_from(p, k, v.at[z_of(4 - k), xy_d, rows_two], 13).wait_recv()
-        ag_copy(p, 16, v, v, sib).start()
+                ag_z_from(p, k, v.at[z_of(4 - k), xy_d, rows_two], 9).wait_recv()
+        ag_copy(p, 12, v, v, sib).start()
 
     def ag_e(p):
         v = weight_piece(p, other)
-        ag_copy(p, 16, v, v, sib).wait_recv()
+        ag_copy(p, 12, v, v, sib).wait_recv()
 
     def ag_f(p):
         v = weight_piece(p, core)
         along_z(lambda k: ag_z(p, k, v.at[zpos, xy]).wait_send())
         pass_to_end(lambda far, k: ag_pass(p, far, k, v.at[far, xy]).wait_send())
-        for k in range(4):
-            ag_x(p, k, v).wait_send()
-            ag_y(p, k, v).wait_send()
+        ag_x(p, 0, v).wait_send()
+        ag_y(p, 0, v).wait_send()
+        three = v.at[pl.ds(0, 3), xy]
+        ag_copy(p, 4, three, three, x_dev).wait_send()
+        ag_copy(p, 6, three, three, y_dev).wait_send()
         ag_one(p, v, sides(p)[0][1]).wait_send()
         if p:
             ag_two(p, v, sides(p)[1][1]).wait_send()
             along_z(lambda k: ag_z2(p, k, v.at[zpos, xy_d, rows_two]).wait_send())
             pass_to_end(
-                lambda far, k: ag_pass(p, far, k, v.at[far, xy_d, rows_two], 13).wait_send()
+                lambda far, k: ag_pass(p, far, k, v.at[far, xy_d, rows_two], 9).wait_send()
             )
-        ag_copy(p, 16, v, v, sib).wait_send()
+        ag_copy(p, 12, v, v, sib).wait_send()
 
     ahead = 3
 
@@ -679,7 +677,7 @@
         return tuple(ring)
 
     def rs_copy(n, i, src, dst, dev):
-        return remote(src, dst, r.rss.at[n, i], r.rsr.at[n, i], dev)
+        return remote(src, dst, r.sent.at[n, i], r.came.at[n, i], dev)
 
     def credit_wait(n, i):
         if RINGS[CREDIT_RINGS[i]] <= n < (PIECES if i in (0, 3, 4) else SHORT):
@@ -761,14 +759,22 @@
         early, late_one, late_two = [], [], []
         if n < SHORT:
             early.append((7, g.at[:, a, rows_two], land.at[0, :, rows_two], a_dev))
-        late_one.append((8, g.at[:, a, one], land.at[0, :, one], a_dev))
-        early.append((9, g.at[:, b, one], land.at[1, :, one], b_dev))
+        late_one.append((7, g.at[:, a, one], land.at[0, :, one], a_dev))
+        early.append((8, g.at[:, b, one], land.at[1, :, one], b_dev))
         if n < SHORT:
             for k in (1, 2, 3):
                 z = z_of(k)
-                early.append((9 + k, g.at[z, b, rows_two], land.at[1, z, rows_two], b_dev))
-            late_two.append((13, g.at[zpos, b, rows_two], land.at[1, zpos, rows_two], b_dev))
+                early.append((8, g.at[z, b, rows_two], land.at[1, z, rows_two], b_dev))
+            late_two.append((8, g.at[zpos, b, rows_two], land.at[1, zpos, rows_two], b_dev))
         return [[rs_copy(n, *entry) for entry in group] for group in (early, late_one, late_two)]
+
+    def rs_all(n):
+        g, land = grad_piece(order[n], core), rs_bufs(n)[2]
+        (a_dev, a), (b_dev, b) = sides(n)
+        return [
+            rs_copy(n, 7, g.at[:, a], land.at[0], a_dev),
+            rs_copy(n, 8, g.at[:, b], land.at[1], b_dev),
+        ]
 
     def rs_one(n):
         p = order[n]
@@ -789,7 +795,7 @@
     def rs_swap(n):
         p = order[n]
         half = pl.ds(pl.multiple_of(other * 24, 8), 24)
-        return rs_copy(n, 18, r.fs.at[p - 1, half], r.fr.at[p - 1], sib)
+        return rs_copy(n, 13, r.fs.at[p - 1, half], r.fr.at[p - 1], sib)
 
     def rs_0(n):
         credit_wait(n, 0)
@@ -811,6 +817,8 @@
         rs_one(n).start()
         if n < SHORT:
             sum_z_start(n, 2, 5, *diagonal(n))
+
+    def rs_early(n):
         credit_wait(n, 3)
         credit_wait(n, 4)
         for copy in rs_main(n)[0]:
@@ -824,10 +832,12 @@
         for z in range(4):
             add_to(g, (z, a, rs_rows_one(n)), l1[z])
         credit_give(n, 1, b_dev)
-        for copy in rs_main(n)[1]:
-            copy.start()
         if n < SHORT:
             sum_z_pass(n, 2, 5, *diagonal(n))
+        else:
+            rs_early(n)
+            for copy in rs_main(n)[1]:
+                copy.start()
 
     def rs_3(n):
         p = order[n]
@@ -838,6 +848,9 @@
             give()
             credit_wait(n, 2)
             rs_two(n).start()
+            rs_early(n)
+            for copy in rs_main(n)[1]:
+                copy.start()
 
     def rs_4(n):
         p = order[n]
@@ -854,30 +867,29 @@
         p = order[n]
         g, l2 = grad_piece(p, core), rs_bufs(n)[2]
         (a_dev, a), (b_dev, b) = sides(n)
-        for group in rs_main(n):
-            for copy in group:
-                copy.wait_recv()
+        for copy in rs_all(n):
+            copy.wait_recv()
         for z in range(4):
             add_to(g, (z, xy), l2[0, z].astype(F32) + l2[1, z].astype(F32))
         credit_give(n, 3, a_dev)
         credit_give(n, 4, b_dev)
         if n < SHORT:
-            sum_z_start(n, 14, 9, *own_line(n))
+            sum_z_start(n, 9, 9, *own_line(n))
         else:
             for k in (1, 2, 3):
-                z_send(n, 14, *own_line(n), k).start()
+                z_send(n, 9, *own_line(n), k).start()
 
     def rs_6(n):
-        sum_z_pass(n, 14, 9, *own_line(n))
+        sum_z_pass(n, 9, 9, *own_line(n))
 
     def rs_7(n):
         p = order[n]
         if n < SHORT:
-            total, give = sum_z_end(n, 14, 9, *own_line(n))
+            total, give = sum_z_end(n, 9, 9, *own_line(n))
         else:
             land = rs_bufs(n)[3]
             for k in (1, 2, 3):
-                z_send(n, 14, *own_line(n), k).wait_recv()
+                z_send(n, 9, *own_line(n), k).wait_recv()
             total = land[0].astype(F32) + land[1].astype(F32) + land[2].astype(F32)
         total = total + grad_piece(p, core)[zpos, xy].astype(F32)
         if p == 0:
@@ -912,29 +924,26 @@
         p = order[n]
         rs_copy(n, 0, grad_piece(p, other), rs_bufs(n)[0], sib).wait_send()
         rs_one(n).wait_send()
-        for group in rs_main(n):
-            for copy in group:
-                copy.wait_send()
+        for copy in rs_all(n):
+            copy.wait_send()
         if n < SHORT:
             sum_z_sent(n, 2, *diagonal(n))
             rs_two(n).wait_send()
-            sum_z_sent(n, 14, *own_line(n))
+            sum_z_sent(n, 9, *own_line(n))
         else:
             for k in (1, 2, 3):
-                z_send(n, 14, *own_line(n), k).wait_send()
+                z_send(n, 9, *own_line(n), k).wait_send()
         if 1 <= p <= 8:
             rs_swap(n).wait_send()
 
-    rs_long = (rs_0, rs_1, rs_2, rs_3, rs_4, rs_5, rs_6, rs_7, rs_8, rs_9)
-    rs_short = (rs_0, rs_1, rs_2, rs_5, rs_7, rs_8, rs_9)
-
-    base = [0, 1, 2, 3, 4, 5, 6, 7, 8, 9, 10, 12, 14]
-
-    def rs_step(s):
+    rs_long = list(zip((rs_0, rs_1, rs_2, rs_3, rs_4, rs_5, rs_6, rs_7, rs_8, rs_9), LONG_AT))
+    rs_short = list(zip((rs_0, rs_1, rs_2, rs_5, rs_7, rs_8, rs_9), SHORT_AT))
+
+    def rs_tick(tick):
         for n in range(PIECES + 1):
-            stages = rs_long if n < SHORT else rs_short
-            if 0 <= s - base[n] < len(stages):
-                stages[s - base[n]](n)
+            for stage, after in rs_long if n < SHORT else rs_short:
+                if STARTS[n] + after == tick:
+                    stage(n)
 
     def rows_of(f):
         return pl.ds(pl.multiple_of(f * WIN, WIN), WIN)
@@ -1086,11 +1095,15 @@
         )
         r.att[rw, head_cols(t, pair)] = (out * scale).astype(BF16)
 
-    def heads_forward(t):
+    def heads_forward(t, between):
         qkv(t)
         for f in range(4):
             for pair in range(2):
                 attention(t, f, pair)
+            if f == 1:
+                for k, tick in enumerate(between):
+                    if tick is not None:
+                        pl.when(t == k)(tick)
 
     def project(f):
         rw = rows_of(f)
@@ -1315,7 +1328,7 @@
     def rs(*numbers):
         def go():
             for s in numbers:
-                rs_step(s)
+                rs_tick(s)
 
         return go
 
@@ -1338,52 +1351,59 @@
     spread_small()
     loop(4, ln1)
     ag_e(1)
-    loop(3, heads_forward, [arrive(2, 4), arrive(3, 5), ag(6)])
-    arrive(4)()
-    loop(4, project, [None, ag(7), None, None])
+    loop(
+        3,
+        functools.partial(heads_forward, between=[ag(4), ag(6), ag(8)]),
+        [arrive(2, 5), arrive(3, 7), arrive(4, 9)],
+    )
+    loop(4, project, [None, ag(10), None, None])
     keep_middle = pltpu.make_async_copy(r.mid, r.ig, r.ld.at[5])
     keep_middle.start()
-    arrive(5)()
-    loop(4, fc1, [arrive(6, 8), arrive(7, 9), arrive(8, 10), ag(11)])
+    ag_e(5)
+    loop(4, fc1, [arrive(6, 11), arrive(7), arrive(8, 12), ag(13)])
     loop(4, turn(1))
-    loop(4, grad_fc2, [ag(12), None, ag(13), ag(14)])
-    rs_step(0)
-    for p in range(PIECES + 1):
-        if p >= 9:
-            ag_e(p)
+    for p in range(9):
         ag_f(p)
-    rs_step(1)
-    loop(4, grad_pre, [None, None, rs(2), None])
-    loop(3, grad_norm_two, [rs(3), None, None])
-    loop(4, grad_fc1, [rs(4), None, None, rs(5)])
+    loop(4, grad_fc2, [None, ag(14), None, None])
+    rs_tick(0)
+    for p in range(9, PIECES + 1):
+        ag_e(p)
+        ag_f(p)
+    loop(4, grad_pre, [rs(1), rs(2), rs(3), rs(4)])
+    loop(3, grad_norm_two, [rs(5), rs(6), rs(7)])
+    loop(4, grad_fc1, [rs(8), rs(9), rs(10), rs(11)])
     keep_middle.wait()
-    loop(4, grad_middle)
+    loop(4, grad_middle, [None, rs(12), None, rs(13)])
     loop(3, grad_proj)
-    rs_step(6)
+    rs_tick(14)
     loop(4, grad_att)
+    rs_tick(15)
     loop(4, turn(0))
-    loop(4, heads_backward(0), [rs(7), None, None, rs(8)])
+    loop(4, heads_backward(0), [rs(16), rs(17), rs(18), rs(19)])
     grad_qkv(0)
-    loop(4, heads_backward(1), [None, rs(9), None, None])
+    rs_tick(20)
+    loop(4, heads_backward(1), [rs(21), rs(22), rs(23), rs(24)])
     grad_qkv(1)
-    rs_step(10)
-    loop(4, heads_backward(2), [None, None, rs(11), None])
+    rs_tick(25)
+    loop(4, heads_backward(2), [rs(26), rs(27), rs(28), rs(29)])
     grad_qkv(2)
-    rs_step(12)
-    loop(3, grad_norm_one, [None, None, rs(13)])
-    loop(4, grad_mixed)
+    rs_tick(30)
+    loop(3, grad_norm_one, [rs(31), rs(32), rs(33)])
+    loop(4, grad_mixed, [None, rs(34), None, rs(35)])
     load_middle = pltpu.make_async_copy(r.ig, r.mid, r.ld.at[6])
     load_middle.start()
     collect_small()
-    rs_step(14)
+    rs_tick(36)
     load_middle.wait()
     write_grad = pltpu.make_async_copy(r.dn, r.ig, r.ld.at[7])
     write_grad.start()
-    loop(3, fc2, [rs(15), rs(16), rs(17)])
+    rs_tick(37)
+    loop(3, fc2, [rs(38, 39), rs(40, 41), rs(42, 43)])
     write_out = pltpu.make_async_copy(r.n2, r.bo, r.ld.at[0])
     write_out.start()
-    for s in range(18, 21):
-        rs_step(s)
+    last = max(at + (LONG_AT if n < SHORT else SHORT_AT)[-1] for n, at in enumerate(STARTS))
+    for tick in range(44, last + 1):
+        rs_tick(tick)
     write_grad.wait()
     write_out.wait()
 

time: 182 us -> 170 us (0.934)
  Pallas kernels: 180 us -> 167 us
    pallas_call x1, Pallas kernels: 173 us -> 161 us  [fused_device(): pl.pallas_call(fused_kernel, out_shape=(shape((1024, 768), BF16), shape((...]
where the time goes in v3:
time: 170 us
  Pallas kernels  167 us (98%)
    pallas_call x1, Pallas kernels, fused_device(): pl.pallas_call(fused_kernel, out_shape=(shape((1024, 768), BF16), shape((...  161 us
    pallas_call x1, Pallas kernels, fused_device(): pl.pallas_call(hand_over, out_shape=tuple((shape(o.shape, o.dtype) for o...  6.35 us

profile of v3, /device:TPU:0, one launch (start us, length us, event | category | flops | bytes accessed | tf_op | source)
XLA Modules:
  0.0 169.8 jit_solution(15509571719742673057)
XLA Ops:
  0.6 1.5 add_bitcast_fusion.refs_4_
  2.1 161.1 %shard_map.280 = (bf16[1024,768]{1,0:T(8,128)(2,1)}, f32[1024,768]{1,0:T(8,128)}, f32[24,2304]{1,0:T(8,128)}, f32[24,768]{1,0:T(8,128)}, f32[24,3072]{1,0:T(8,12...) custom-call(bf16[1024,768]{1,0:T(8,128)(2,1)} %refs_0_.1, bf16[1024,768]{1,0:T(8,128)(2,1)} %refs_1_.1, s32[8,128]{1,0:T(8,128)} %bitcast.12, ...), custom_call_target="tpu_custom_call" | custom-call | tf_op jit(solution)/shard_map/pallas_call | solution.py:1475
  163.2 6.4 %shard_map.281 = (bf16[1024,768]{1,0:T(8,128)(2,1)}, f32[1024,768]{1,0:T(8,128)}, f32[24,2304]{1,0:T(8,128)}, f32[24,768]{1,0:T(8,128)}, f32[24,3072]{1,0:T(8,12...) custom-call(bf16[1024,768]{1,0:T(8,128)(2,1)} %get-tuple-element.37., ...), custom_call_target="tpu_custom_call" | custom-call | tf_op jit(solution)/shard_map/pallas_call | solution.py:1503

commit v4 on v3

--- a/solution.py
+++ b/solution.py
@@ -322,8 +322,10 @@
 RINGS = dict(l0=2, l1=4, lz=4, lt=4, l2=4, l3=4)
 CREDIT_RINGS = ["l0", "l1", "lt", "l2", "l2"] + ["lz"] * 4 + ["l3"] * 4
 SHORT = 11
+DIRECT = 1
 LONG_AT = (0, 2, 5, 8, 11, 14, 17, 20, 22, 23)
 SHORT_AT = (0, 2, 5, 8, 11, 13, 14)
+SMALL_AT = (0, 1, 3, 5, 7, 8, 9)
 STARTS = (0, 1, 3, 5, 8, 10, 13, 16, 19, 22, 25, 30, 36)
 MESH_ID = pl.DeviceIdType.MESH
 
@@ -402,7 +404,7 @@
     hact=((1024, 3072), BF16),
     gp=((11, 768, COLS), BF16),
     dn=((1024, 768), F32),
-    lse=((24, 8, 256), F32),
+    lse=((48, 256), F32),
     wa=((8, 768, COLS), BF16),
     w1=((8, 768, COLS), BF16),
     w2=((8, 768, COLS), BF16),
@@ -417,8 +419,8 @@
     lt=((RINGS["lt"], ROWS - CUT, COLS), BF16),
     l2=((RINGS["l2"], 2, 4, ROWS, COLS), BF16),
     l3=((RINGS["l3"], 4, ROWS, COLS), BF16),
-    l1s=((4, ROWS, COLS), BF16),
-    l3s=((4, ROWS, COLS), BF16),
+    l1s=((PIECES - SHORT, 4, ROWS, COLS), BF16),
+    l3s=((PIECES - SHORT, 3, ROWS, COLS), BF16),
     s0=((4, 4, 8, LANES), F32),
     s1=((4, 8, LANES), F32),
     s2=((2, 4, 8, LANES), F32),
@@ -524,14 +526,19 @@
     at_start, at_end = zpos == 0, zpos == 3
     inside = jnp.logical_and(zpos > 0, zpos < 3)
 
-    def along_z(fn):
-        pl.when(jnp.logical_not(at_end))(lambda: fn(1))
-        fn(2)
-        pl.when(jnp.logical_not(at_start))(lambda: fn(3))
-
-    def pass_to_end(fn):
-        pl.when(zpos == 1)(lambda: fn(3, 3))
-        pl.when(zpos == 2)(lambda: fn(0, 1))
+    def along_z(p, fn):
+        if p < DIRECT:
+            for k in (1, 2, 3):
+                fn(k)
+        else:
+            pl.when(jnp.logical_not(at_end))(lambda: fn(1))
+            fn(2)
+            pl.when(jnp.logical_not(at_start))(lambda: fn(3))
+
+    def pass_to_end(p, fn):
+        if p >= DIRECT:
+            pl.when(zpos == 1)(lambda: fn(3, 3))
+            pl.when(zpos == 2)(lambda: fn(0, 1))
 
     def ag_z(p, k, at):
         return ag_copy(p, k - 1, at, at, z_dev(k))
@@ -571,7 +578,7 @@
 
     def ag_a(p):
         v = weight_piece(p, core)
-        along_z(lambda k: ag_z(p, k, v.at[zpos, xy]).start())
+        along_z(p, lambda k: ag_z(p, k, v.at[zpos, xy]).start())
         ag_x(p, 0, v).start()
         ag_y(p, 0, v).start()
 
@@ -585,7 +592,7 @@
     def ag_b2(p):
         v = weight_piece(p, core)
         ag_z_from(p, 2, v.at[z_of(2), xy]).wait_recv()
-        pass_to_end(lambda far, k: ag_pass(p, far, k, v.at[far, xy]).start())
+        pass_to_end(p, lambda far, k: ag_pass(p, far, k, v.at[far, xy]).start())
         ag_x(p, 2, v).start()
         ag_y(p, 2, v).start()
 
@@ -599,7 +606,7 @@
         if p:
             v = weight_piece(p, core)
             ag_two(p, v, xy_d).wait_recv()
-            along_z(lambda k: ag_z2(p, k, v.at[zpos, xy_d, rows_two]).start())
+            along_z(p, lambda k: ag_z2(p, k, v.at[zpos, xy_d, rows_two]).start())
 
     def ag_c1(p):
         v = weight_piece(p, core)
@@ -612,7 +619,7 @@
             v = weight_piece(p, core)
             ag_z_from(p, 2, v.at[z_of(2), xy_d, rows_two], 9).wait_recv()
             pass_to_end(
-                lambda far, k: ag_pass(p, far, k, v.at[far, xy_d, rows_two], 9).start()
+                p, lambda far, k: ag_pass(p, far, k, v.at[far, xy_d, rows_two], 9).start()
             )
 
     def ag_d(p):
@@ -632,8 +639,8 @@
 
     def ag_f(p):
         v = weight_piece(p, core)
-        along_z(lambda k: ag_z(p, k, v.at[zpos, xy]).wait_send())
-        pass_to_end(lambda far, k: ag_pass(p, far, k, v.at[far, xy]).wait_send())
+        along_z(p, lambda k: ag_z(p, k, v.at[zpos, xy]).wait_send())
+        pass_to_end(p, lambda far, k: ag_pass(p, far, k, v.at[far, xy]).wait_send())
         ag_x(p, 0, v).wait_send()
         ag_y(p, 0, v).wait_send()
         three = v.at[pl.ds(0, 3), xy]
@@ -642,9 +649,9 @@
         ag_one(p, v, sides(p)[0][1]).wait_send()
         if p:
             ag_two(p, v, sides(p)[1][1]).wait_send()
-            along_z(lambda k: ag_z2(p, k, v.at[zpos, xy_d, rows_two]).wait_send())
+            along_z(p, lambda k: ag_z2(p, k, v.at[zpos, xy_d, rows_two]).wait_send())
             pass_to_end(
-                lambda far, k: ag_pass(p, far, k, v.at[far, xy_d, rows_two], 9).wait_send()
+                p, lambda far, k: ag_pass(p, far, k, v.at[far, xy_d, rows_two], 9).wait_send()
             )
         ag_copy(p, 12, v, v, sib).wait_send()
 
@@ -673,7 +680,7 @@
             return r.s0, r.s1, r.s2, r.s3
         ring = [getattr(r, name).at[n % RINGS[name]] for name in ("l0", "l1", "l2", "l3")]
         if n >= SHORT:
-            ring[1], ring[3] = r.l1s, r.l3s
+            ring[1], ring[3] = r.l1s.at[n - SHORT], r.l3s.at[n - SHORT]
         return tuple(ring)
 
     def rs_copy(n, i, src, dst, dev):
@@ -939,9 +946,11 @@
     rs_long = list(zip((rs_0, rs_1, rs_2, rs_3, rs_4, rs_5, rs_6, rs_7, rs_8, rs_9), LONG_AT))
     rs_short = list(zip((rs_0, rs_1, rs_2, rs_5, rs_7, rs_8, rs_9), SHORT_AT))
 
+    rs_small = list(zip((rs_0, rs_1, rs_2, rs_5, rs_7, rs_8, rs_9), SMALL_AT))
+
     def rs_tick(tick):
         for n in range(PIECES + 1):
-            for stage, after in rs_long if n < SHORT else rs_short:
+            for stage, after in rs_long if n < SHORT else rs_short if n < PIECES else rs_small:
                 if STARTS[n] + after == tick:
                     stage(n)
 
@@ -1085,7 +1094,7 @@
         log_total = row_max + jnp.log(total)
         for h in range(2):
             col = jnp.broadcast_to(log_total[WIN * h : WIN * (h + 1)], (WIN, 8))
-            r.lse[f * 6 + 2 * t + pair, h : h + 1, :] = jnp.transpose(col)[0:1]
+            r.lse[pl.ds(f * 12 + 4 * t + 2 * pair + h, 1), :] = jnp.transpose(col)[0:1]
         e = e.astype(BF16)
         out = dot_nn(jnp.concatenate([e[:WIN], e[WIN:]], axis=1), two_heads(v2))
         scale = jnp.where(
@@ -1213,8 +1222,8 @@
         k2 = r.packed[rw, part(t, 1, pair)]
         v2 = r.packed[rw, part(t, 2, pair)]
         qs, ds, ks = two_heads(q2), two_heads(r.n2[rw, head_cols(t, pair)]), two_heads(k2)
-        at = f * 6 + 2 * t + pair
-        log_total = jnp.concatenate([r.lse[at, 0:1, :], r.lse[at, 1:2, :]], axis=1)
+        at = f * 12 + 4 * t + 2 * pair
+        log_total = jnp.concatenate([r.lse[pl.ds(at + h, 1), :] for h in range(2)], axis=1)
         probs = jnp.exp(dot_nt(k2, qs) - log_total)
         prod = probs * dot_nt(v2, ds)
         row_dot = jnp.sum(prod, axis=0, keepdims=True)

time: 170 us -> 169 us (level)
  no operation moved by 1% of the time
where the time goes in v4:
time: 169 us
  Pallas kernels  167 us (99%)
    pallas_call x1, Pallas kernels, fused_device(): pl.pallas_call(fused_kernel, out_shape=(shape((1024, 768), BF16), shape((...  160 us
    pallas_call x1, Pallas kernels, fused_device(): pl.pallas_call(hand_over, out_shape=tuple((shape(o.shape, o.dtype) for o...  6.35 us

profile of v4, /device:TPU:0, one launch (start us, length us, event | category | flops | bytes accessed | tf_op | source)
XLA Modules:
  0.0 168.9 jit_solution(841127202132783257)
XLA Ops:
  0.6 1.5 add_bitcast_fusion.refs_4_
  2.1 160.3 %shard_map.280 = (bf16[1024,768]{1,0:T(8,128)(2,1)}, f32[1024,768]{1,0:T(8,128)}, f32[24,2304]{1,0:T(8,128)}, f32[24,768]{1,0:T(8,128)}, f32[24,3072]{1,0:T(8,12...) custom-call(bf16[1024,768]{1,0:T(8,128)(2,1)} %refs_0_.1, bf16[1024,768]{1,0:T(8,128)(2,1)} %refs_1_.1, s32[8,128]{1,0:T(8,128)} %bitcast.12, ...), custom_call_target="tpu_custom_call" | custom-call | tf_op jit(solution)/shard_map/pallas_call | solution.py:1484
  162.4 6.4 %shard_map.281 = (bf16[1024,768]{1,0:T(8,128)(2,1)}, f32[1024,768]{1,0:T(8,128)}, f32[24,2304]{1,0:T(8,128)}, f32[24,768]{1,0:T(8,128)}, f32[24,3072]{1,0:T(8,12...) custom-call(bf16[1024,768]{1,0:T(8,128)(2,1)} %get-tuple-element.37., ...), custom_call_target="tpu_custom_call" | custom-call | tf_op jit(solution)/shard_map/pallas_call | solution.py:1512

commit v5 on v4

--- a/solution.py
+++ b/solution.py
@@ -326,7 +326,7 @@
 LONG_AT = (0, 2, 5, 8, 11, 14, 17, 20, 22, 23)
 SHORT_AT = (0, 2, 5, 8, 11, 13, 14)
 SMALL_AT = (0, 1, 3, 5, 7, 8, 9)
-STARTS = (0, 1, 3, 5, 8, 10, 13, 16, 19, 22, 25, 30, 36)
+STARTS = (0, 2, 4, 6, 9, 11, 14, 17, 20, 23, 26, 30, 36)
 MESH_ID = pl.DeviceIdType.MESH
 
 

time: 169 us -> 171 us (1.012)
  Pallas kernels: 167 us -> 169 us
    pallas_call x1, Pallas kernels: 160 us -> 162 us  [fused_device(): pl.pallas_call(fused_kernel, out_shape=(shape((1024, 768), BF16), shape((...]
where the time goes in v5:
time: 171 us
  Pallas kernels  169 us (99%)
    pallas_call x1, Pallas kernels, fused_device(): pl.pallas_call(fused_kernel, out_shape=(shape((1024, 768), BF16), shape((...  162 us
    pallas_call x1, Pallas kernels, fused_device(): pl.pallas_call(hand_over, out_shape=tuple((shape(o.shape, o.dtype) for o...  6.35 us

profile of v5, /device:TPU:0, one launch (start us, length us, event | category | flops | bytes accessed | tf_op | source)
XLA Modules:
  0.0 171.0 jit_solution(17563018622326135144)
XLA Ops:
  0.6 1.5 add_bitcast_fusion.refs_4_
  2.1 162.4 %shard_map.280 = (bf16[1024,768]{1,0:T(8,128)(2,1)}, f32[1024,768]{1,0:T(8,128)}, f32[24,2304]{1,0:T(8,128)}, f32[24,768]{1,0:T(8,128)}, f32[24,3072]{1,0:T(8,12...) custom-call(bf16[1024,768]{1,0:T(8,128)(2,1)} %refs_0_.1, bf16[1024,768]{1,0:T(8,128)(2,1)} %refs_1_.1, s32[8,128]{1,0:T(8,128)} %bitcast.12, ...), custom_call_target="tpu_custom_call" | custom-call | tf_op jit(solution)/shard_map/pallas_call | solution.py:1484
  164.5 6.4 %shard_map.281 = (bf16[1024,768]{1,0:T(8,128)(2,1)}, f32[1024,768]{1,0:T(8,128)}, f32[24,2304]{1,0:T(8,128)}, f32[24,768]{1,0:T(8,128)}, f32[24,3072]{1,0:T(8,12...) custom-call(bf16[1024,768]{1,0:T(8,128)(2,1)} %get-tuple-element.37., ...), custom_call_target="tpu_custom_call" | custom-call | tf_op jit(solution)/shard_map/pallas_call | solution.py:1512
